TPU v7x, 512 devices: a whole 4x8x8 slice. The times are simulated.
512 devices in a mesh: gx: 32 (over x, z), gy: 16 (over y, core).
Axes of the slice: x: 4, y: 8, z: 8, core: 2. Of those that a mesh axis runs over, the one named last changes fastest.
Arguments:
- features: bfloat16 [32, 131072], P(None, ('gx', 'gy')), may hold values from -6 to 6
- offsets: bfloat16 [3, 131072], P(None, ('gx', 'gy')), may hold values from 0 to 16
- point_cell: int32 [131072], P(('gx', 'gy')), may hold values from 0 to 511
- tile_owner: int32 [1024, 4], P(('gx', 'gy')), may hold values from 0 to 15, all different within a row; in each aligned block of 2 rows (0 to 1, 2 to 3, ...) at most 2 rows name the same one
- tile_local: int32 [1024, 4], P(('gx', 'gy')), may hold values from 0 to 31
- live_count: int32 [1024], P(('gx', 'gy')), may hold values from 1 to 4
- w_first: bfloat16 [64, 3], replicated, may hold values from -3.5 to 3.5
- b_first: float32 [64], replicated, may hold values from -3 to 3
- w_second: bfloat16 [64, 64], replicated, may hold values from -0.75 to 0.75
- b_second: float32 [64], replicated, may hold values from -3 to 3
- w_third: bfloat16 [32, 64], replicated, may hold values from -0.75 to 0.75
- w_point: bfloat16 [32, 32], replicated, may hold values from -1 to 1
- b_point: float32 [32], replicated, may hold values from -3 to 3
- w_modes: bfloat16 [32, 32, 32, 2, 32, 32], P(None, 'gx', 'gy'), may hold values from -3 to 3
Outputs:
- latent_out: float32 [128, 128, 32, 128], P('gx', 'gy')
Inputs may be any that keep to these rules, and one draw needn't show every extreme that they name: `tile_owner`: each row names 4 different owners; among the rows of one device no owner is named by more than 2 rows.
All inputs are finite; a program needn't handle non-finite values.
Results may differ from a plain program's by a relative error of at most 0.0015.
Values may be sent and summed in bfloat16 or wider, within the bound.
No kernel may reach another device: no remote copies, remote signals or barrier semaphores. Data moves between devices by JAX's collectives and lax.ppermute only.
A program may use at most 64 MiB of HBM per device.

v0:
```python
import functools
import math

import jax
import jax.numpy as jnp
import numpy as np
from jax import lax
from jax.experimental import pallas as pl
from jax.experimental.pallas import tpu as pltpu
from jax.sharding import PartitionSpec as P

NZ = 128
CX = 4
CY = 8
SPAN = 16
PB = 128
C = 32
HID = 64
N_GX = 32
N_GY = 16
BLK = 2
LIST = 4
PAIRS = BLK * LIST
MODES = 32
UNROLL = 4
F32 = jnp.float32
BF16 = jnp.bfloat16
BEST = lax.Precision.HIGHEST
NN = (((1,), (0,)), ((), ()))
NT = (((1,), (1,)), ((), ()))
TN = (((0,), (0,)), ((), ()))
HALF_PI = (1.5703125, 4.837512969970703125e-4, 7.549789954891882e-8)
SIN_TERMS = (-1.9515295891e-4, 8.3321608736e-3, -1.6666654611e-1)
COS_TERMS = (2.443315711809948e-5, -1.388731625493765e-3, 4.166664568298827e-2)
GELU_A = math.sqrt(2.0 / math.pi)
GELU_B = GELU_A * 0.044715


def iota(shape, dim):
    return lax.broadcasted_iota(jnp.int32, shape, dim)


def dot(a, b, dims=NN):
    return lax.dot_general(a, b, dims, preferred_element_type=F32)


def fine_dot(a, b, dims=NN):
    return lax.dot_general(a, b, dims, precision=BEST, preferred_element_type=F32)


def halves(x):
    high = x.astype(BF16)
    return high, (x - high.astype(F32)).astype(BF16)


def sin_cos(x):
    count = jnp.floor(x * (2.0 / math.pi) + 0.5)
    rest = x - count * HALF_PI[0]
    rest = rest - count * HALF_PI[1]
    rest = rest - count * HALF_PI[2]
    square = rest * rest
    s = (SIN_TERMS[0] * square + SIN_TERMS[1]) * square + SIN_TERMS[2]
    s = s * square * rest + rest
    c = (COS_TERMS[0] * square + COS_TERMS[1]) * square + COS_TERMS[2]
    c = c * square * square - 0.5 * square + 1.0
    quarter = count.astype(jnp.int32)
    odd = (quarter & 1) != 0
    sine = jnp.where(odd, c, s)
    cosine = jnp.where(odd, s, c)
    sine = jnp.where((quarter & 2) != 0, -sine, sine)
    cosine = jnp.where(((quarter + 1) & 2) != 0, -cosine, cosine)
    return sine, cosine


def angles(length, two_sided):
    orders = np.arange(MODES)
    frequency = np.where(orders < MODES // 2, orders, length - MODES + orders) if two_sided else orders
    turns = np.arange(length)[:, None] * frequency[None, :] % length
    return turns * (2.0 * math.pi / length)


def f32(x):
    return np.ascontiguousarray(x, dtype=np.float32)


def split_table(x):
    high = f32(x).astype(jnp.bfloat16)
    low = (x - high.astype(np.float64)).astype(np.float32).astype(jnp.bfloat16)
    return high, low


def tables(size_x, size_y):
    scale = 1.0 / math.sqrt(size_x * size_y * NZ)
    along_z = angles(NZ, False)
    both = np.stack([np.cos(along_z), -np.sin(along_z)], -1) * scale
    both = both.reshape(NZ, N_GY, 4)
    forward_z = f32(both.transpose(2, 1, 0).reshape(4 * N_GY, NZ))
    inverse_z = np.concatenate(split_table(both.reshape(NZ, 4 * N_GY).T), 1)
    along_y = angles(size_y, True)
    per_row = np.repeat(along_y.T, CX, axis=0)
    phase_y = np.concatenate(split_table(np.cos(per_row)) + split_table(np.sin(per_row)), 0)
    back_y = f32(np.concatenate([np.cos(along_y), np.sin(along_y)], 1))
    along_x = angles(size_x, True)
    forward_x = f32(np.concatenate([np.cos(along_x), np.sin(along_x)], 0).T.reshape(MODES, 2 * size_x))
    back_x = f32(np.concatenate([np.cos(along_x), np.sin(along_x)], 1))
    return forward_z, inverse_z, phase_y, back_y, forward_x, back_x


def pair_kernel(
    owner, tile, live, feats, offs, cells, rows, w2, w3, wp, fz,
    modes_out, cells_out,
    cz, sz, w2b, w3b, side, point, feat, sin_p, cos_p, sums, held,
):
    gx = lax.axis_index("gx")
    gy = lax.axis_index("gy")
    pick = ((iota((4 * HID, HID), 0) & (HID - 1)) == iota((4 * HID, HID), 1)).astype(BF16)
    spread = dot(dot(pick, w2[...], NT).astype(BF16), pick, NT)
    same = (iota(spread.shape, 0) // HID) == (iota(spread.shape, 1) // HID)
    w2b[...] = jnp.where(same, spread, 0.0).astype(BF16)
    pick_c = ((iota((4 * C, C), 0) & (C - 1)) == iota((4 * C, C), 1)).astype(BF16)
    spread = dot(dot(pick, w3[...], NT).astype(BF16), pick_c, NT)
    same = (iota(spread.shape, 0) // HID) == (iota(spread.shape, 1) // C)
    w3b[...] = jnp.where(same, 0.5 * spread, 0.0).astype(BF16)
    side[...] = fine_dot(rows[...], pick.astype(F32), NT)
    cell_z = ((iota((NZ // 4, 4 * HID), 1) // HID) * (NZ // 4) + iota((NZ // 4, 4 * HID), 0)).astype(F32)
    sine, cosine = sin_cos(side[2:3, :] * cell_z)
    cz[...] = cosine
    sz[...] = sine
    sums[...] = jnp.zeros_like(sums)
    cells_out[...] = jnp.zeros_like(cells_out)
    row_of = iota((PB, PB), 0)
    for b in range(BLK):
        span = slice(b * PB, (b + 1) * PB)
        q = cells[:, span]
        place = [
            ((q // 64) * SPAN).astype(F32) + offs[0:1, span].astype(F32),
            ((q // 8 % 8) * SPAN).astype(F32) + offs[1:2, span].astype(F32),
            ((q % 8) * SPAN).astype(F32) + offs[2:3, span].astype(F32),
        ]
        stack = jnp.where(row_of == 0, place[0], jnp.where(row_of == 1, place[1], place[2]))
        turned = jnp.transpose(stack)
        point[b] = (
            turned[:, 0:1] * side[0:1, :PB] + turned[:, 1:2] * side[1:2, :PB] + turned[:, 2:3] * side[2:3, :PB]
        )
        block = feats[:, span].astype(F32) * (1.0 / math.sqrt(PB))
        feat[b] = jnp.transpose(jnp.concatenate([block] * 4, axis=0))
    for b in range(BLK):

        def one_pair(s, carry, b=b):
            t = tile[b, s]
            x = (CX * gx + t // CY).astype(F32)
            y = (CY * owner[b, s] + t % CY).astype(F32)
            line = side[0:1, :PB] * x + side[1:2, :PB] * y + side[3:4, :PB]
            sine, cosine = sin_cos(line - point[b])
            sin_p[...] = sine
            cos_p[...] = cosine

            def some_cells(i, carry):
                for u in range(UNROLL):
                    g = i * UNROLL + u
                    c = cz[pl.ds(g, 1), :]
                    d = sz[pl.ds(g, 1), :]
                    sp = sin_p[...]
                    cp = cos_p[...]
                    first = jnp.concatenate(
                        [sp * c[:, :PB] + cp * d[:, :PB], sp * c[:, PB:] + cp * d[:, PB:]], axis=1
                    ).astype(BF16)
                    h = dot(first, w2b[...]) + side[4:5, :]
                    th = jnp.tanh(h * (GELU_B * (h * h) + GELU_A))
                    second = (h + h * th).astype(BF16)
                    kern = dot(second, w3b[...])
                    total = jnp.sum(kern * feat[b], axis=0, keepdims=True)
                    sums[pl.ds((b * LIST + s) * (NZ // 4) + g, 1), :] = total
                return carry

            lax.fori_loop(0, NZ // 4 // UNROLL, some_cells, 0)
            return carry

        lax.fori_loop(0, live[b], one_pair, 0)
    shape = (4 * C, 16 * C)
    copy_c = (
        ((iota(shape, 0) & (C - 1)) == (iota(shape, 1) & (C - 1))) & ((iota(shape, 0) // C) == (iota(shape, 1) // (4 * C)))
    ).astype(BF16)
    high, low = halves(sums[...])
    wide = dot(high, copy_c) + dot(low, copy_c)
    by_cell = [
        jnp.concatenate([wide[j * 32 : (j + 1) * 32, k * 128 : (k + 1) * 128] for k in range(4)], axis=0)
        for j in range(PAIRS)
    ]
    eye = (iota((C, 4 * C), 0) == iota((C, 4 * C), 1)).astype(BF16)
    wpt = dot(wp[...], eye, TN).astype(BF16)
    lane_group = iota((N_GY, 4 * C), 1) // C
    held[...] = jnp.zeros_like(held)
    for j in range(PAIRS):
        b, s = divmod(j, LIST)
        full = fine_dot(fz[...], by_cell[j])
        picked = jnp.zeros((N_GY, 4 * C), F32)
        for g in range(4):
            picked = jnp.where(lane_group == g, full[g * N_GY : (g + 1) * N_GY], picked)
        held[:, j, :] = picked
        high, low = halves(by_cell[j])
        mapped = dot(wpt, high, NT) + dot(wpt, low, NT)

        @pl.when(s < live[b])
        def _(b=b, s=s, mapped=mapped):
            cells_out[owner[b, s], b * C : (b + 1) * C, :] = mapped.astype(cells_out.dtype)

    lane = iota((1, 128), 1)
    xs = jnp.zeros((1, 128), jnp.int32)
    ys = jnp.zeros((1, 128), jnp.int32)
    on = jnp.zeros((1, 128), jnp.int32)
    for j in range(PAIRS):
        b, s = divmod(j, LIST)
        here = lane == gy * PAIRS + j
        t = tile[b, s]
        xs = jnp.where(here, t // CY, xs)
        ys = jnp.where(here, CY * owner[b, s] + t % CY, ys)
        on = jnp.where(here & (s < live[b]), 1, on)
    for k, v in enumerate((xs, ys, on)):
        held[:, PAIRS + k, :] = jnp.broadcast_to(v.astype(F32), (N_GY, 128))
    modes_out[...] = held[...].astype(modes_out.dtype)


def y_kernel(got, phase, out, slots):
    gy = lax.axis_index("gy")
    full = got[...].astype(F32)
    values = full[:, :PAIRS, :].reshape(N_GY * PAIRS, 128)
    extra = full[:, PAIRS:, :]
    sent = jnp.sum(extra, axis=0)
    xs, ys, on = sent[0:1], sent[1:2], sent[2:3]
    square = (128, 128)
    hot = ((iota(square, 0).astype(F32) == ys) & (on > 0.5)).astype(BF16)
    turned = dot(phase[...], hot)
    here = (iota(square, 0) & (CX - 1)).astype(F32) == xs
    cosine = jnp.where(here, turned[0:128] + turned[128:256], 0.0)
    sine = jnp.where(here, turned[256:384] + turned[384:512], 0.0)
    result = fine_dot(cosine, values) + fine_dot(sine, rotated(values, 1.0))
    out[...] = result.reshape(MODES, CX, 128).astype(out.dtype)
    yi = ys.astype(jnp.int32)
    mine = ((yi // CY) == gy) & (on > 0.5)
    number = jnp.where(mine, xs.astype(jnp.int32) * CY + (yi & (CY - 1)) + 1, 0).astype(BF16)
    group = ((iota(square, 0) // LIST) == iota(square, 1)).astype(BF16)
    slots[...] = dot(jnp.broadcast_to(number, (8, 128)), group).astype(jnp.int32) - 1


def rotated(x, sign):
    up = pltpu.roll(x, 128 - C, 1)
    down = pltpu.roll(x, C, 1)
    real = ((iota(x.shape, 1) // C) & 1) == 0
    return jnp.where(real, sign * up, -sign * down)


def x_kernel(got, weights, forward, back, out):
    size_x = CX * N_GX
    values = got[...].astype(F32).reshape(size_x, 128)
    spectrum = fine_dot(forward[:, :size_x], values) + fine_dot(forward[:, size_x:], rotated(values, 1.0))
    parts = [spectrum if g == 0 else pltpu.roll(spectrum, 128 - g * C, 1) for g in range(4)]
    high, low = halves(jnp.concatenate(parts, axis=0))
    spread = ((iota((128, C * C), 1) // C) == iota((128, C * C), 0)).astype(BF16)
    wide = dot(high, spread) + dot(low, spread)
    totals = []
    for k in range(2):
        real = wide[(2 * k) * MODES : (2 * k + 1) * MODES]
        imag = wide[(2 * k + 1) * MODES : (2 * k + 2) * MODES]
        sum_r = jnp.zeros((MODES, 128), F32)
        sum_i = jnp.zeros((MODES, 128), F32)
        for j in range(C * C // 128):
            lanes = slice(j * 128, (j + 1) * 128)
            at = (2 * k) * C * C + j * 128
            wr = weights[:, at : at + 128].astype(F32)
            wi = weights[:, at + C * C : at + C * C + 128].astype(F32)
            sum_r = sum_r + real[:, lanes] * wr - imag[:, lanes] * wi
            sum_i = sum_i + real[:, lanes] * wi + imag[:, lanes] * wr
        for v in (sum_r, sum_i):
            v = v + pltpu.roll(v, 64, 1)
            totals.append(v + pltpu.roll(v, 32, 1))
    group = iota((MODES, 128), 1) // C
    r0, i0, r1, i1 = totals
    mixed = jnp.where(group == 0, r0, jnp.where(group == 1, i0, jnp.where(group == 2, r1, i1)))
    other = jnp.where(group == 0, -i0, jnp.where(group == 1, r0, jnp.where(group == 2, -i1, r1)))
    result = fine_dot(back[...], jnp.concatenate([mixed, other], axis=0))
    out[...] = result.reshape(N_GX, CX, 128).astype(out.dtype)


def back_kernel(got, back, out):
    lines = [got[:, x, :].astype(F32) for x in range(CX)]
    group = iota((MODES, 128), 1) // C
    turned = []
    for g in range(4):
        line = jnp.zeros((MODES, 128), F32)
        for x in range(CX):
            shift = ((x - g) * C) % 128
            moved = lines[x] if shift == 0 else pltpu.roll(lines[x], shift, 1)
            line = jnp.where(group == x, moved, line)
        turned.append(line)
    size_y = CY * N_GY
    for k in range(2):
        real, imag = turned[2 * k], turned[2 * k + 1]
        stack = jnp.concatenate(
            [jnp.concatenate([real, imag], axis=1), jnp.concatenate([-imag, real], axis=1)], axis=0
        )
        result = fine_dot(back[...], stack)
        for g in range(2):
            piece = result[:, g * 128 : (g + 1) * 128].reshape(N_GY, CY, 128)
            at = (2 * k + g) * CY
            out[:, at : at + CY, :] = piece.astype(out.dtype)


def end_kernel(slots, got, cells, inverse, bias, out, wide, total):
    wide[...] = got[...].astype(F32).reshape(N_GY * 4 * CY, 128)
    column = jnp.broadcast_to(bias[...], (C, NZ))
    for y in range(CY):
        values = wide[pl.ds(y, 4 * N_GY, stride=CY), :].astype(BF16)
        both = dot(values, inverse[...], TN)
        line = both[:, :NZ] + both[:, NZ:]
        for x in range(CX):
            total[x * CY + y] = line[x * C : (x + 1) * C] + column
    for n in range(N_GY * BLK):
        src, b = divmod(n, BLK)
        t = slots[0, n]

        @pl.when(t >= 0)
        def _(src=src, b=b, t=t):
            total[t] = total[t] + cells[src, b * C : (b + 1) * C, :].astype(F32)

    for t in range(CX * CY):
        h = total[t]
        th = jnp.tanh(h * (GELU_B * (h * h) + GELU_A))
        out[t // CY, t % CY] = 0.5 * (h + h * th)


def call(kernel, out_shape, in_specs, scratch=(), flops=0, size=0):
    return pl.pallas_call(
        kernel,
        out_shape=out_shape,
        in_specs=in_specs,
        scratch_shapes=list(scratch),
        compiler_params=pltpu.CompilerParams(vmem_limit_bytes=40 * 1024 * 1024),
        cost_estimate=pl.CostEstimate(flops=flops, bytes_accessed=size, transcendentals=0),
    )


VM = pl.BlockSpec(memory_space=pltpu.VMEM)
SM = pl.BlockSpec(memory_space=pltpu.SMEM)


def local(
    features, offsets, point_cell, tile_owner, tile_local, live_count,
    w_first, b_first, w_second, b_second, w_third, w_point, b_point, w_modes,
):
    forward_z, inverse_z, phase_y, back_y, forward_x, back_x = tables(CX * N_GX, CY * N_GY)
    rows = jnp.concatenate(
        [w_first.astype(F32).T, b_first[None], b_second[None], jnp.zeros((3, HID), F32)], axis=0
    )
    vm = pltpu.VMEM
    modes, mapped = call(
        pair_kernel,
        (
            jax.ShapeDtypeStruct((N_GY, 16, 128), BF16),
            jax.ShapeDtypeStruct((N_GY, BLK * C, NZ), BF16),
        ),
        [SM, SM, SM] + [VM] * 8,
        [
            vm((NZ // 4, 4 * HID), F32), vm((NZ // 4, 4 * HID), F32),
            vm((4 * HID, 4 * HID), BF16), vm((4 * HID, 4 * C), BF16),
            vm((8, 4 * HID), F32), vm((BLK, PB, PB), F32), vm((BLK, PB, PB), F32),
            vm((PB, PB), F32), vm((PB, PB), F32),
            vm((PAIRS * NZ // 4, 4 * C), F32), vm((N_GY, 16, 128), F32),
        ],
        flops=1_600_000_000, size=1_000_000,
    )(
        tile_owner, tile_local, live_count, features, offsets, point_cell.reshape(1, -1),
        rows, w_second, w_third, w_point, forward_z,
    )
    modes = lax.all_to_all(modes, "gy", 0, 0, tiled=True)
    mapped = lax.all_to_all(mapped, "gy", 0, 0, tiled=True)
    along_y, slots = call(
        y_kernel,
        (jax.ShapeDtypeStruct((MODES, CX, 128), F32), jax.ShapeDtypeStruct((8, 128), jnp.int32)),
        [VM, VM],
        flops=100_000_000, size=500_000,
    )(modes, phase_y)
    along_y = lax.all_to_all(along_y, "gx", 0, 0, tiled=True)
    lines = call(
        x_kernel,
        jax.ShapeDtypeStruct((N_GX, CX, 128), F32),
        [VM] * 4,
        flops=100_000_000, size=500_000,
    )(along_y, w_modes.reshape(MODES, -1), forward_x, back_x)
    lines = lax.all_to_all(lines, "gx", 0, 0, tiled=True)
    cells = call(
        back_kernel,
        jax.ShapeDtypeStruct((N_GY, 4 * CY, 128), BF16),
        [VM] * 2,
        flops=100_000_000, size=500_000,
    )(lines, back_y)
    cells = lax.all_to_all(cells, "gy", 0, 0, tiled=True)
    return call(
        end_kernel,
        jax.ShapeDtypeStruct((CX, CY, C, NZ), F32),
        [SM] + [VM] * 4,
        [vm((N_GY * 4 * CY, 128), F32), vm((CX * CY, C, NZ), F32)],
        flops=100_000_000, size=1_000_000,
    )(slots, cells, mapped, inverse_z, b_point.reshape(C, 1))


def solution(mesh):
    both = ("gx", "gy")
    return jax.shard_map(
        local,
        mesh=mesh,
        in_specs=(
            P(None, both), P(None, both), P(both), P(both, None), P(both, None), P(both),
            P(), P(), P(), P(), P(), P(), P(),
            P(None, "gx", "gy", None, None, None),
        ),
        out_specs=P("gx", "gy", None, None),
        check_vma=False,
    )
```

profile of v0, /device:TPU:1, one launch (start us, length us, event | category | flops | bytes accessed | tf_op | source)
XLA Modules:
  0.0 130.8 jit_solution(6284234910202798446)
XLA Ops:
  0.0 0.0 copy-start.3
  0.0 0.7 convert_bitcast_fusion
  0.7 0.1 pad.3.clone
  0.8 0.0 copy-start.7
  0.8 0.8 maximum_maximum_fusion.rows
  1.5 0.0 copy-start.8
  1.5 0.0 copy-start.11
  1.5 0.0 copy-done.3
  1.5 0.0 copy-done.7
  1.5 0.7 copy-done.8
  2.2 0.0 copy-done.11
  2.2 0.0 copy-start.4
  2.2 0.7 copy-done.4
  2.9 0.0 copy-start.5
  2.9 0.7 copy-done.5
  3.6 0.0 copy-start.6
  3.6 0.7 copy-done.6
  4.3 0.0 copy-start.9
  4.3 0.7 copy-done.9
  5.0 0.0 copy-start.10
  5.0 0.7 copy-done.10
  5.7 0.0 copy-start.13
  5.7 0.8 copy-done.13
  6.4 0.0 copy-start.14
  6.4 22.3 %shard_map.190 = (bf16[16,16,128]{2,1,0:T(8,128)(2,1)S(1)}, bf16[16,64,128]{2,1,0:T(8,128)(2,1)}) custom-call(s32[2,4]{1,0:T(2,128)S(1)} %copy-done.8, s32[2,4]{1,0:T(2,128)S(1)} %copy-done.9, s32[2]{0:T(128)S(1)} %copy-done.11, bf16[32,256]{1,0:T(8,128)(2,1)S(1)} %copy-done.3, bf16[3,256]{1,0:T(4,128)(2,1)S(1)} %copy-done.7, s32[1,256]{1,0:T(1,128)S(1)} %bitcast.8, ...), custom_call_target="tpu_custom_call" | custom-call | flops 1600000000 | bytes 1000000 | tf_op jit(solution)/shard_map/pallas_call | solution.py:356
  28.8 0.0 copy-start.12
  28.8 34.0 %all_to_all.25.got = bf16[16,16,128]{2,1,0:T(8,128)(2,1)S(1)} all-to-all(bf16[16,16,128]{2,1,0:T(8,128)(2,1)S(1)} %get-tuple-element.9), channel_id=1, replica_groups=mesh['gx'=32,'gy'=16] {'gy'}, dimensions={0} | all-to-all | bytes 131072 | tf_op jit(solution)/shard_map/all_to_all | solution.py:375
  62.8 0.0 copy-done.12
  62.8 1.1 shard_map.191
  63.9 12.8 %all-to-all-start.1 = ((f32[32,4,128]{2,1,0:T(4,128)}), f32[32,4,128]{2,1,0:T(4,128)S(1)}, u32[]{:S(2)}, u32[]{:S(2)}) async-start(f32[32,4,128]{2,1,0:T(4,128)} %get-tuple-element.11), calls=%async_computation.1 | async-start | bytes 131072 | tf_op jit(solution)/shard_map/all_to_all | solution.py:383
  76.7 0.0 copy-done.14
  76.8 0.0 copy-start
  76.8 0.0 copy-start.1
  76.8 1.2 reshape.10.weights
  77.9 7.7 %all-to-all-done.1.got = f32[32,4,128]{2,1,0:T(4,128)S(1)} async-done(((f32[32,4,128]{2,1,0:T(4,128)}), f32[32,4,128]{2,1,0:T(4,128)S(1)}, u32[]{:S(2)}, u32[]{:S(2)}) %all-to-all-start.1) | async-done | bytes 65568 | tf_op jit(solution)/shard_map/all_to_all | solution.py:383
  85.6 0.0 copy-done
  85.6 0.0 copy-done.1
  85.6 1.2 shard_map.192
  86.8 12.0 %all_to_all.26.got = f32[32,4,128]{2,1,0:T(4,128)S(1)} all-to-all(f32[32,4,128]{2,1,0:T(4,128)S(1)} %shard_map.192), channel_id=1, replica_groups=mesh['gx'=32,'gy'=16] {'gx'}, dimensions={0} | all-to-all | bytes 131072 | tf_op jit(solution)/shard_map/all_to_all | solution.py:390
  98.8 6.1 %all-to-all-start.4 = ((bf16[16,64,128]{2,1,0:T(8,128)(2,1)}), bf16[16,64,128]{2,1,0:T(8,128)(2,1)S(1)}, u32[]{:S(2)}, u32[]{:S(2)}) async-start(bf16[16,64,128]{2,1,0:T(8,128)(2,1)} %get-tuple-element.12), calls=%async_computation.4 | async-start | bytes 524288 | tf_op jit(solution)/shard_map/all_to_all | solution.py:376
  104.9 1.1 shard_map.193
  106.0 10.7 %all-to-all-done.4.cells = bf16[16,64,128]{2,1,0:T(8,128)(2,1)S(1)} async-done(((bf16[16,64,128]{2,1,0:T(8,128)(2,1)}), bf16[16,64,128]{2,1,0:T(8,128)(2,1)S(1)}, u32[]{:S(2)}, u32[]{:S(2)}) %all-to-all-start.4) | async-done | bytes 262176 | tf_op jit(solution)/shard_map/all_to_all | solution.py:376
  116.8 0.0 copy-start.2
  116.8 3.5 %all-to-all-start.3 = ((bf16[16,32,128]{2,1,0:T(8,128)(2,1)}), bf16[16,32,128]{2,1,0:T(8,128)(2,1)S(1)}, u32[]{:S(2)}, u32[]{:S(2)}) async-start(bf16[16,32,128]{2,1,0:T(8,128)(2,1)} %shard_map.193), calls=%async_computation.3 | async-start | bytes 262144 | tf_op jit(solution)/shard_map/all_to_all | solution.py:397
  120.3 0.0 copy-start.15
  120.3 0.6 copy-done.15
  121.0 0.1 copy.21.bias
  121.1 7.6 %all-to-all-done.3.got = bf16[16,32,128]{2,1,0:T(8,128)(2,1)S(1)} async-done(((bf16[16,32,128]{2,1,0:T(8,128)(2,1)}), bf16[16,32,128]{2,1,0:T(8,128)(2,1)S(1)}, u32[]{:S(2)}, u32[]{:S(2)}) %all-to-all-start.3) | async-done | bytes 131104 | tf_op jit(solution)/shard_map/all_to_all | solution.py:397
  128.7 0.0 copy-done.2
  128.7 2.1 %shard_map.194 = f32[4,8,32,128]{3,2,1,0:T(8,128)} custom-call(s32[8,128]{1,0:T(8,128)S(1)} %get-tuple-element.10.slots, bf16[16,32,128]{2,1,0:T(8,128)(2,1)S(1)} %all-to-all-done.3.got, bf16[16,64,128]{2,1,0:T(8,128)(2,1)S(1)} %all-to-all-done.4.cells, bf16[64,256]{1,0:T(8,128)(2,1)S(1)} %copy-done.2, f32[32,1]{1,0:T(8,128)S(1)} %copy.21.bias), custom_call_target="tpu_custom_call" | custom-call | flops 100000000 | bytes 1000000 | tf_op jit(solution)/shard_map/pallas_call | solution.py:398
  (1 shorter events, 0.0 us)
Async XLA Ops:
  0.0 1.5 %copy-start.3 = (bf16[32,256]{1,0:T(8,128)(2,1)S(1)}, bf16[32,256]{1,0:T(8,128)(2,1)}, u32[]{:S(2)}) copy-start(bf16[32,256]{1,0:T(8,128)(2,1)} %feats.1) | copy-start | bytes 49156
  0.8 0.8 copy-start.7
  1.5 0.7 copy-start.8
  1.5 0.7 copy-start.11
  2.2 0.7 copy-start.4
  2.9 0.7 copy-start.5
  3.6 0.7 copy-start.6
  4.3 0.7 copy-start.9
  5.0 0.7 copy-start.10
  5.7 0.8 copy-start.13
  6.4 70.3 %copy-start.14 = (bf16[32,1,2,2,32,32]{5,4,3,2,1,0:T(8,128)(2,1)S(1)}, bf16[32,1,2,2,32,32]{5,4,3,2,1,0:T(8,128)(2,1)}, u32[]{:S(2)}) copy-start(bf16[32,1,2,2,32,32]{5,4,3,2,1,0:T(8,128)(2,1)} %param.33) | copy-start | bytes 786436
  28.8 34.0 %copy-start.12 = (bf16[512,128]{1,0:T(8,128)(2,1)S(1)}, bf16[512,128]{1,0:T(8,128)(2,1)}, u32[]{:S(2)}) copy-start(bf16[512,128]{1,0:T(8,128)(2,1)} %constant.13.clone.phase) | copy-start | bytes 393220
  63.9 21.7 %all-to-all-start.1 = ((f32[32,4,128]{2,1,0:T(4,128)}), f32[32,4,128]{2,1,0:T(4,128)S(1)}, u32[]{:S(2)}, u32[]{:S(2)}) async-start(f32[32,4,128]{2,1,0:T(4,128)} %get-tuple-element.11), calls=%async_computation.1 | async-start | bytes 131072 | tf_op jit(solution)/shard_map/all_to_all | solution.py:383
  76.8 8.9 %copy-start = (f32[128,64]{1,0:T(8,128)S(1)}, f32[128,64]{1,0:T(8,128)}, u32[]{:S(2)}) copy-start(f32[128,64]{1,0:T(8,128)} %constant.15.clone.back) | copy-start | bytes 98308
  76.8 8.8 %copy-start.1 = (f32[32,256]{1,0:T(8,128)S(1)}, f32[32,256]{1,0:T(8,128)}, u32[]{:S(2)}) copy-start(f32[32,256]{1,0:T(8,128)} %constant.14.clone.forward) | copy-start | bytes 98308
  98.8 17.9 %all-to-all-start.4 = ((bf16[16,64,128]{2,1,0:T(8,128)(2,1)}), bf16[16,64,128]{2,1,0:T(8,128)(2,1)S(1)}, u32[]{:S(2)}, u32[]{:S(2)}) async-start(bf16[16,64,128]{2,1,0:T(8,128)(2,1)} %get-tuple-element.12), calls=%async_computation.4 | async-start | bytes 524288 | tf_op jit(solution)/shard_map/all_to_all | solution.py:376
  116.8 11.9 %copy-start.2 = (bf16[64,256]{1,0:T(8,128)(2,1)S(1)}, bf16[64,256]{1,0:T(8,128)(2,1)}, u32[]{:S(2)}) copy-start(bf16[64,256]{1,0:T(8,128)(2,1)} %constant.16.clone.inverse) | copy-start | bytes 98308
  116.8 11.9 %all-to-all-start.3 = ((bf16[16,32,128]{2,1,0:T(8,128)(2,1)}), bf16[16,32,128]{2,1,0:T(8,128)(2,1)S(1)}, u32[]{:S(2)}, u32[]{:S(2)}) async-start(bf16[16,32,128]{2,1,0:T(8,128)(2,1)} %shard_map.193), calls=%async_computation.3 | async-start | bytes 262144 | tf_op jit(solution)/shard_map/all_to_all | solution.py:397
  120.3 0.7 copy-start.15
where the time goes:
time: 132 us; the launch traced here: 131 us
  blocking collectives  46 us (35%)
  Pallas kernels  27.9 us (21%)
  waiting for transfers between devices  26 us (20%)
  starting transfers between devices  22.5 us (17%)
  local copies, waits for them, and re-layouts  6.91 us (5%)
  other arithmetic  1.45 us (1%)
    all_to_all x1, blocking collectives, local(): modes = lax.all_to_all(modes, 'gy', 0, 0, tiled=True)  34 us
    pallas_call x1, Pallas kernels, local(): call(pair_kernel, (jax.ShapeDtypeStruct((N_GY, 16, 128), BF16), jax.Shape...  22.3 us
    all_to_all x1, starting transfers between devices, local(): along_y = lax.all_to_all(along_y, 'gx', 0, 0, tiled=True)  12.8 us
    all_to_all x1, blocking collectives, local(): lines = lax.all_to_all(lines, 'gx', 0, 0, tiled=True)  12 us
    all_to_all x1, waiting for transfers between devices, local(): mapped = lax.all_to_all(mapped, 'gy', 0, 0, tiled=True)  10.7 us
    all_to_all x1, waiting for transfers between devices, local(): along_y = lax.all_to_all(along_y, 'gx', 0, 0, tiled=True)  7.65 us
    all_to_all x1, waiting for transfers between devices, local(): cells = lax.all_to_all(cells, 'gy', 0, 0, tiled=True)  7.59 us
    all_to_all x1, starting transfers between devices, local(): mapped = lax.all_to_all(mapped, 'gy', 0, 0, tiled=True)  6.07 us
  transfers between devices with their start and end apart: 3, of which 3 were waited for; matrix products, arithmetic and copies ran while one was open for 1% of the time, Pallas kernels for 1%

commit v1 on v0

--- a/solution.py
+++ b/solution.py
@@ -22,7 +22,9 @@
 LIST = 4
 PAIRS = BLK * LIST
 MODES = 32
-UNROLL = 4
+UNROLL = 1
+STACK = 32
+VMEM_ONE = 62 * 1024 * 1024
 F32 = jnp.float32
 BF16 = jnp.bfloat16
 BEST = lax.Precision.HIGHEST
@@ -94,7 +96,7 @@
     along_z = angles(NZ, False)
     both = np.stack([np.cos(along_z), -np.sin(along_z)], -1) * scale
     both = both.reshape(NZ, N_GY, 4)
-    forward_z = f32(both.transpose(2, 1, 0).reshape(4 * N_GY, NZ))
+    forward_z = np.concatenate(split_table(both.transpose(2, 1, 0).reshape(4 * N_GY, NZ)), 0)
     inverse_z = np.concatenate(split_table(both.reshape(NZ, 4 * N_GY).T), 1)
     along_y = angles(size_y, True)
     per_row = np.repeat(along_y.T, CX, axis=0)
@@ -107,9 +109,9 @@
 
 
 def pair_kernel(
-    owner, tile, live, feats, offs, cells, rows, w2, w3, wp, fz,
-    modes_out, cells_out,
-    cz, sz, w2b, w3b, side, point, feat, sin_p, cos_p, sums, held,
+    owner, tile, live, feats, offs, cells, w1, b1, b2, w2, w3, fz,
+    modes_out, sums,
+    cz, sz, w2b, w3b, side, point, feat, sin_p, cos_p, held,
 ):
     gx = lax.axis_index("gx")
     gy = lax.axis_index("gy")
@@ -121,13 +123,16 @@
     spread = dot(dot(pick, w3[...], NT).astype(BF16), pick_c, NT)
     same = (iota(spread.shape, 0) // HID) == (iota(spread.shape, 1) // C)
     w3b[...] = jnp.where(same, 0.5 * spread, 0.0).astype(BF16)
-    side[...] = fine_dot(rows[...], pick.astype(F32), NT)
+    shape = (HID, 4 * HID)
+    pick_t = (iota(shape, 0) == (iota(shape, 1) & (HID - 1))).astype(F32)
+    side[0:3, :] = fine_dot(w1[...].astype(F32), pick_t)
+    side[3:4, :] = fine_dot(jnp.broadcast_to(b1[...], (8, HID)), pick_t)[0:1]
+    side[4:5, :] = fine_dot(jnp.broadcast_to(b2[...], (8, HID)), pick_t)[0:1]
     cell_z = ((iota((NZ // 4, 4 * HID), 1) // HID) * (NZ // 4) + iota((NZ // 4, 4 * HID), 0)).astype(F32)
     sine, cosine = sin_cos(side[2:3, :] * cell_z)
     cz[...] = cosine
     sz[...] = sine
     sums[...] = jnp.zeros_like(sums)
-    cells_out[...] = jnp.zeros_like(cells_out)
     row_of = iota((PB, PB), 0)
     for b in range(BLK):
         span = slice(b * PB, (b + 1) * PB)
@@ -157,54 +162,43 @@
 
             def some_cells(i, carry):
                 for u in range(UNROLL):
-                    g = i * UNROLL + u
-                    c = cz[pl.ds(g, 1), :]
-                    d = sz[pl.ds(g, 1), :]
+                    g = (i * UNROLL + u) * STACK
                     sp = sin_p[...]
                     cp = cos_p[...]
-                    first = jnp.concatenate(
-                        [sp * c[:, :PB] + cp * d[:, :PB], sp * c[:, PB:] + cp * d[:, PB:]], axis=1
-                    ).astype(BF16)
-                    h = dot(first, w2b[...]) + side[4:5, :]
+                    lines = []
+                    for k in range(STACK):
+                        c = cz[pl.ds(g + k, 1), :]
+                        d = sz[pl.ds(g + k, 1), :]
+                        lines.append(
+                            jnp.concatenate(
+                                [sp * c[:, :PB] + cp * d[:, :PB], sp * c[:, PB:] + cp * d[:, PB:]], axis=1
+                            ).astype(BF16)
+                        )
+                    h = dot(jnp.concatenate(lines, axis=0), w2b[...]) + side[4:5, :]
                     th = jnp.tanh(h * (GELU_B * (h * h) + GELU_A))
                     second = (h + h * th).astype(BF16)
                     kern = dot(second, w3b[...])
-                    total = jnp.sum(kern * feat[b], axis=0, keepdims=True)
-                    sums[pl.ds((b * LIST + s) * (NZ // 4) + g, 1), :] = total
+                    for k in range(STACK):
+                        total = jnp.sum(kern[k * PB : (k + 1) * PB] * feat[b], axis=0, keepdims=True)
+                        sums[pl.ds((b * LIST + s) * (NZ // 4) + g + k, 1), :] = total
                 return carry
 
-            lax.fori_loop(0, NZ // 4 // UNROLL, some_cells, 0)
+            lax.fori_loop(0, NZ // 4 // (UNROLL * STACK), some_cells, 0)
             return carry
 
         lax.fori_loop(0, live[b], one_pair, 0)
-    shape = (4 * C, 16 * C)
-    copy_c = (
-        ((iota(shape, 0) & (C - 1)) == (iota(shape, 1) & (C - 1))) & ((iota(shape, 0) // C) == (iota(shape, 1) // (4 * C)))
-    ).astype(BF16)
-    high, low = halves(sums[...])
-    wide = dot(high, copy_c) + dot(low, copy_c)
-    by_cell = [
-        jnp.concatenate([wide[j * 32 : (j + 1) * 32, k * 128 : (k + 1) * 128] for k in range(4)], axis=0)
-        for j in range(PAIRS)
-    ]
-    eye = (iota((C, 4 * C), 0) == iota((C, 4 * C), 1)).astype(BF16)
-    wpt = dot(wp[...], eye, TN).astype(BF16)
+    by_cell = spread_cells(sums[...])
     lane_group = iota((N_GY, 4 * C), 1) // C
     held[...] = jnp.zeros_like(held)
+    table = fz[...]
     for j in range(PAIRS):
-        b, s = divmod(j, LIST)
-        full = fine_dot(fz[...], by_cell[j])
+        high, low = by_cell[0][j], by_cell[1][j]
+        both = dot(table, high)
+        full = both[: 4 * N_GY] + both[4 * N_GY :] + dot(table[: 4 * N_GY], low)
         picked = jnp.zeros((N_GY, 4 * C), F32)
         for g in range(4):
             picked = jnp.where(lane_group == g, full[g * N_GY : (g + 1) * N_GY], picked)
         held[:, j, :] = picked
-        high, low = halves(by_cell[j])
-        mapped = dot(wpt, high, NT) + dot(wpt, low, NT)
-
-        @pl.when(s < live[b])
-        def _(b=b, s=s, mapped=mapped):
-            cells_out[owner[b, s], b * C : (b + 1) * C, :] = mapped.astype(cells_out.dtype)
-
     lane = iota((1, 128), 1)
     xs = jnp.zeros((1, 128), jnp.int32)
     ys = jnp.zeros((1, 128), jnp.int32)
@@ -219,6 +213,37 @@
     for k, v in enumerate((xs, ys, on)):
         held[:, PAIRS + k, :] = jnp.broadcast_to(v.astype(F32), (N_GY, 128))
     modes_out[...] = held[...].astype(modes_out.dtype)
+
+
+def spread_cells(sums):
+    shape = (4 * C, 16 * C)
+    copy_c = (
+        ((iota(shape, 0) & (C - 1)) == (iota(shape, 1) & (C - 1))) & ((iota(shape, 0) // C) == (iota(shape, 1) // (4 * C)))
+    ).astype(BF16)
+    terms = []
+    for term in halves(sums):
+        wide = dot(term, copy_c).astype(BF16)
+        terms.append(
+            [
+                jnp.concatenate([wide[j * 32 : (j + 1) * 32, k * 128 : (k + 1) * 128] for k in range(4)], axis=0)
+                for j in range(PAIRS)
+            ]
+        )
+    return terms
+
+
+def map_kernel(owner, live, sums, wp, out):
+    high, low = spread_cells(sums[...])
+    eye = (iota((C, 4 * C), 0) == iota((C, 4 * C), 1)).astype(BF16)
+    wpt = dot(wp[...], eye, TN).astype(BF16)
+    out[...] = jnp.zeros_like(out)
+    for j in range(PAIRS):
+        b, s = divmod(j, LIST)
+        mapped = dot(wpt, high[j], NT) + dot(wpt, low[j], NT)
+
+        @pl.when(s < live[b])
+        def _(b=b, s=s, mapped=mapped):
+            out[owner[b, s], b * C : (b + 1) * C, :] = mapped.astype(out.dtype)
 
 
 def y_kernel(got, phase, out, slots):
@@ -282,7 +307,8 @@
     out[...] = result.reshape(N_GX, CX, 128).astype(out.dtype)
 
 
-def back_kernel(got, back, out):
+def back_kernel(got, back, held, out):
+    out[:, 4 * CY :, :] = held[...]
     lines = [got[:, x, :].astype(F32) for x in range(CX)]
     group = iota((MODES, 128), 1) // C
     turned = []
@@ -306,8 +332,8 @@
             out[:, at : at + CY, :] = piece.astype(out.dtype)
 
 
-def end_kernel(slots, got, cells, inverse, bias, out, wide, total):
-    wide[...] = got[...].astype(F32).reshape(N_GY * 4 * CY, 128)
+def end_kernel(slots, got, inverse, bias, out, wide, total):
+    wide[...] = got[:, : 4 * CY, :].astype(F32).reshape(N_GY * 4 * CY, 128)
     column = jnp.broadcast_to(bias[...], (C, NZ))
     for y in range(CY):
         values = wide[pl.ds(y, 4 * N_GY, stride=CY), :].astype(BF16)
@@ -321,7 +347,8 @@
 
         @pl.when(t >= 0)
         def _(src=src, b=b, t=t):
-            total[t] = total[t] + cells[src, b * C : (b + 1) * C, :].astype(F32)
+            at = 4 * CY + b * C
+            total[t] = total[t] + got[src, at : at + C, :].astype(F32)
 
     for t in range(CX * CY):
         h = total[t]
@@ -329,51 +356,64 @@
         out[t // CY, t % CY] = 0.5 * (h + h * th)
 
 
-def call(kernel, out_shape, in_specs, scratch=(), flops=0, size=0):
+def call(kernel, out_shape, in_specs, scratch=(), flops=0, size=0, vmem=40 * 1024 * 1024):
     return pl.pallas_call(
         kernel,
         out_shape=out_shape,
         in_specs=in_specs,
         scratch_shapes=list(scratch),
-        compiler_params=pltpu.CompilerParams(vmem_limit_bytes=40 * 1024 * 1024),
+        compiler_params=pltpu.CompilerParams(vmem_limit_bytes=vmem),
         cost_estimate=pl.CostEstimate(flops=flops, bytes_accessed=size, transcendentals=0),
     )
 
 
 VM = pl.BlockSpec(memory_space=pltpu.VMEM)
 SM = pl.BlockSpec(memory_space=pltpu.SMEM)
+
+
+def stage_one(
+    features, offsets, point_cell, tile_owner, tile_local, live_count,
+    w_first, b_first, w_second, b_second, w_third, *_,
+):
+    forward_z = tables(CX * N_GX, CY * N_GY)[0]
+    vm = pltpu.VMEM
+    return call(
+        pair_kernel,
+        (
+            jax.ShapeDtypeStruct((N_GY, 16, 128), BF16),
+            jax.ShapeDtypeStruct((PAIRS * NZ // 4, 4 * C), F32),
+        ),
+        [SM, SM, SM] + [VM] * 9,
+        [
+            vm((NZ // 4, 4 * HID), F32), vm((NZ // 4, 4 * HID), F32),
+            vm((4 * HID, 4 * HID), BF16), vm((4 * HID, 4 * C), BF16),
+            vm((8, 4 * HID), F32), vm((BLK, PB, PB), F32), vm((BLK, PB, PB), F32),
+            vm((PB, PB), F32), vm((PB, PB), F32), vm((N_GY, 16, 128), F32),
+        ],
+        flops=1_600_000_000, size=1_000_000, vmem=VMEM_ONE,
+    )(
+        tile_owner, tile_local, live_count, features, offsets, point_cell.reshape(1, -1),
+        w_first.T, b_first.reshape(1, -1), b_second.reshape(1, -1), w_second, w_third, forward_z,
+    )
 
 
 def local(
     features, offsets, point_cell, tile_owner, tile_local, live_count,
     w_first, b_first, w_second, b_second, w_third, w_point, b_point, w_modes,
 ):
-    forward_z, inverse_z, phase_y, back_y, forward_x, back_x = tables(CX * N_GX, CY * N_GY)
-    rows = jnp.concatenate(
-        [w_first.astype(F32).T, b_first[None], b_second[None], jnp.zeros((3, HID), F32)], axis=0
-    )
+    _, inverse_z, phase_y, back_y, forward_x, back_x = tables(CX * N_GX, CY * N_GY)
     vm = pltpu.VMEM
-    modes, mapped = call(
-        pair_kernel,
-        (
-            jax.ShapeDtypeStruct((N_GY, 16, 128), BF16),
-            jax.ShapeDtypeStruct((N_GY, BLK * C, NZ), BF16),
-        ),
-        [SM, SM, SM] + [VM] * 8,
-        [
-            vm((NZ // 4, 4 * HID), F32), vm((NZ // 4, 4 * HID), F32),
-            vm((4 * HID, 4 * HID), BF16), vm((4 * HID, 4 * C), BF16),
-            vm((8, 4 * HID), F32), vm((BLK, PB, PB), F32), vm((BLK, PB, PB), F32),
-            vm((PB, PB), F32), vm((PB, PB), F32),
-            vm((PAIRS * NZ // 4, 4 * C), F32), vm((N_GY, 16, 128), F32),
-        ],
-        flops=1_600_000_000, size=1_000_000,
-    )(
-        tile_owner, tile_local, live_count, features, offsets, point_cell.reshape(1, -1),
-        rows, w_second, w_third, w_point, forward_z,
+    modes, sums = stage_one(
+        features, offsets, point_cell, tile_owner, tile_local, live_count,
+        w_first, b_first, w_second, b_second, w_third,
     )
     modes = lax.all_to_all(modes, "gy", 0, 0, tiled=True)
-    mapped = lax.all_to_all(mapped, "gy", 0, 0, tiled=True)
+    mapped = call(
+        map_kernel,
+        jax.ShapeDtypeStruct((N_GY, BLK * C, NZ), BF16),
+        [SM, SM] + [VM] * 2,
+        flops=100_000_000, size=1_000_000,
+    )(tile_owner, live_count, sums, w_point)
     along_y, slots = call(
         y_kernel,
         (jax.ShapeDtypeStruct((MODES, CX, 128), F32), jax.ShapeDtypeStruct((8, 128), jnp.int32)),
@@ -390,18 +430,18 @@
     lines = lax.all_to_all(lines, "gx", 0, 0, tiled=True)
     cells = call(
         back_kernel,
-        jax.ShapeDtypeStruct((N_GY, 4 * CY, 128), BF16),
-        [VM] * 2,
+        jax.ShapeDtypeStruct((N_GY, 4 * CY + BLK * C, NZ), BF16),
+        [VM] * 3,
         flops=100_000_000, size=500_000,
-    )(lines, back_y)
+    )(lines, back_y, mapped)
     cells = lax.all_to_all(cells, "gy", 0, 0, tiled=True)
     return call(
         end_kernel,
         jax.ShapeDtypeStruct((CX, CY, C, NZ), F32),
-        [SM] + [VM] * 4,
+        [SM] + [VM] * 3,
         [vm((N_GY * 4 * CY, 128), F32), vm((CX * CY, C, NZ), F32)],
         flops=100_000_000, size=1_000_000,
-    )(slots, cells, mapped, inverse_z, b_point.reshape(C, 1))
+    )(slots, cells, inverse_z, b_point.reshape(C, 1))
 
 
 def solution(mesh):

time: 132 us -> 97.9 us (0.74)
  blocking collectives: 46 us -> 16 us
  local copies, waits for them, and re-layouts: 6.91 us -> 2.53 us
  starting transfers between devices: 22.5 us -> 25 us
  Pallas kernels: 27.9 us -> 26.4 us
  other arithmetic: 1.45 us -> 0 us
  waiting for transfers between devices: 26 us -> 27.4 us
    all_to_all x1, blocking collectives: 34 us -> 16 us  [local(): modes = lax.all_to_all(modes, 'gy', 0, 0, tiled=True)]
    all_to_all x1 -> x0, blocking collectives: 12 us -> none  [local(): lines = lax.all_to_all(lines, 'gx', 0, 0, tiled=True)]
    all_to_all x1, waiting for transfers between devices: 7.59 us -> 13.8 us  [local(): cells = lax.all_to_all(cells, 'gy', 0, 0, tiled=True)]
    all_to_all x1, waiting for transfers between devices: 10.7 us -> 5.91 us  [local(): lines = lax.all_to_all(lines, 'gx', 0, 0, tiled=True)]
    unnamed x32 -> x20, local copies, waits for them, and re-layouts: 5.58 us -> 1.33 us
    all_to_all x1, starting transfers between devices: 3.54 us -> 6.23 us  [local(): cells = lax.all_to_all(cells, 'gy', 0, 0, tiled=True)]
    pallas_call x2 -> x3, Pallas kernels: 23.4 us -> 21.3 us  [the longest x1 17.8 us: stage_one(): call(pair_kernel, (jax.ShapeDtypeStruct((N_GY, 16, 128), BF16), jax.Shape...]
    all_to_all x1, starting transfers between devices: 6.07 us -> 3.99 us  [local(): lines = lax.all_to_all(lines, 'gx', 0, 0, tiled=True)]
  transfers between devices with their start and end apart: 3 -> 3, of which waited for: 3 -> 3; matrix products, arithmetic and copies ran while one was open for 1% -> 1% of each run, Pallas kernels for 1% -> 2%
where the time goes in v1:
time: 97.9 us; the launch traced here: 97.4 us
  waiting for transfers between devices  27.4 us (28%)
  Pallas kernels  26.4 us (27%)
  starting transfers between devices  25 us (26%)
  blocking collectives  16 us (16%)
  local copies, waits for them, and re-layouts  2.53 us (3%)
    pallas_call x1, Pallas kernels, stage_one(): call(pair_kernel, (jax.ShapeDtypeStruct((N_GY, 16, 128), BF16), jax.Shape...  17.8 us
    all_to_all x1, blocking collectives, local(): modes = lax.all_to_all(modes, 'gy', 0, 0, tiled=True)  16 us
    all_to_all x1, starting transfers between devices, local(): along_y = lax.all_to_all(along_y, 'gx', 0, 0, tiled=True)  14.8 us
    all_to_all x1, waiting for transfers between devices, local(): cells = lax.all_to_all(cells, 'gy', 0, 0, tiled=True)  13.8 us
    all_to_all x1, waiting for transfers between devices, local(): along_y = lax.all_to_all(along_y, 'gx', 0, 0, tiled=True)  7.71 us
    all_to_all x1, starting transfers between devices, local(): cells = lax.all_to_all(cells, 'gy', 0, 0, tiled=True)  6.23 us
    all_to_all x1, waiting for transfers between devices, local(): lines = lax.all_to_all(lines, 'gx', 0, 0, tiled=True)  5.91 us
    all_to_all x1, starting transfers between devices, local(): lines = lax.all_to_all(lines, 'gx', 0, 0, tiled=True)  3.99 us
  transfers between devices with their start and end apart: 3, of which 3 were waited for; matrix products, arithmetic and copies ran while one was open for 1% of the time, Pallas kernels for 2%

profile of v1, /device:TPU:1, one launch (start us, length us, event | category | flops | bytes accessed | tf_op | source)
XLA Modules:
  0.0 97.4 jit_solution(2758035980574584789)
XLA Ops:
  0.0 0.0 copy-start.8
  0.0 17.8 %shard_map.190 = (bf16[16,16,128]{2,1,0:T(8,128)(2,1)}, f32[256,128]{1,0:T(8,128)}) custom-call(s32[2,4]{1,0:T(2,128)} %owner.3, s32[2,4]{1,0:T(2,128)} %tile.1, s32[2]{0:T(128)} %live.3, bf16[32,256]{1,0:T(8,128)(2,1)} %feats.1, bf16[3,256]{1,0:T(4,128)(2,1)} %offs.1, s32[1,256]{1,0:T(1,128)} %bitcast.8, bf16[3,64]{1,0:T(4,128)(2,1)} %bitcast.9, ...), custom_call_target="tpu_custom_call" | custom-call | flops 1600000000 | bytes 1000000 | tf_op jit(solution)/shard_map/pallas_call | solution.py:380
  17.8 0.0 copy-start.7
  17.8 16.0 %all_to_all.20.got = bf16[16,16,128]{2,1,0:T(8,128)(2,1)S(1)} all-to-all(bf16[16,16,128]{2,1,0:T(8,128)(2,1)} %get-tuple-element.9), channel_id=1, replica_groups=mesh['gx'=32,'gy'=16] {'gy'}, dimensions={0} | all-to-all | bytes 131072 | tf_op jit(solution)/shard_map/all_to_all | solution.py:410
  33.8 0.0 copy-done.7
  33.8 1.1 %shard_map.191 = (f32[32,4,128]{2,1,0:T(4,128)}, s32[8,128]{1,0:T(8,128)S(1)}) custom-call(bf16[16,16,128]{2,1,0:T(8,128)(2,1)S(1)} %all_to_all.20.got, bf16[512,128]{1,0:T(8,128)(2,1)S(1)} %copy-done.7), custom_call_target="tpu_custom_call" | custom-call | flops 100000000 | bytes 500000 | tf_op jit(solution)/shard_map/pallas_call | solution.py:417
  34.9 14.8 %all-to-all-start.1 = ((f32[32,4,128]{2,1,0:T(4,128)}), f32[32,4,128]{2,1,0:T(4,128)S(1)}, u32[]{:S(2)}, u32[]{:S(2)}) async-start(f32[32,4,128]{2,1,0:T(4,128)} %get-tuple-element.11), calls=%async_computation.1 | async-start | bytes 131072 | tf_op jit(solution)/shard_map/all_to_all | solution.py:423
  49.7 0.0 copy-done.8
  49.7 0.0 copy-start
  49.7 0.0 copy-start.2
  49.8 1.1 %reshape.18.weights = bf16[32,4096]{1,0:T(8,128)(2,1)S(1)} reshape(bf16[32,1,2,2,32,32]{5,4,3,2,1,0:T(8,128)(2,1)S(1)} %copy-done.8) | data formatting | bytes 524288 | tf_op jit(solution)/shard_map/reshape | solution.py:429
  50.9 7.7 %all-to-all-done.1.got = f32[32,4,128]{2,1,0:T(4,128)S(1)} async-done(((f32[32,4,128]{2,1,0:T(4,128)}), f32[32,4,128]{2,1,0:T(4,128)S(1)}, u32[]{:S(2)}, u32[]{:S(2)}) %all-to-all-start.1) | async-done | bytes 65568 | tf_op jit(solution)/shard_map/all_to_all | solution.py:423
  58.6 0.0 copy-done
  58.6 0.0 copy-done.2
  58.6 0.0 copy-start.4
  58.6 1.8 %shard_map.192 = f32[32,4,128]{2,1,0:T(4,128)} custom-call(f32[32,4,128]{2,1,0:T(4,128)S(1)} %all-to-all-done.1.got, bf16[32,4096]{1,0:T(8,128)(2,1)S(1)} %reshape.18.weights, f32[32,256]{1,0:T(8,128)S(1)} %copy-done.2, f32[128,64]{1,0:T(8,128)S(1)} %copy-done), custom_call_target="tpu_custom_call" | custom-call | flops 100000000 | bytes 500000 | tf_op jit(solution)/shard_map/pallas_call | solution.py:424
  60.4 0.0 copy-start.1
  60.4 4.0 %all-to-all-start.2 = ((f32[32,4,128]{2,1,0:T(4,128)}), f32[32,4,128]{2,1,0:T(4,128)S(1)}, u32[]{:S(2)}, u32[]{:S(2)}) async-start(f32[32,4,128]{2,1,0:T(4,128)} %shard_map.192), calls=%async_computation.2 | async-start | bytes 131072 | tf_op jit(solution)/shard_map/all_to_all | solution.py:430
  64.4 0.0 copy-start.5
  64.4 0.0 copy-start.6
  64.5 0.0 copy-done.4
  64.5 0.0 copy-done.1
  64.5 0.6 copy-done.5
  65.1 0.0 copy-done.6
  65.1 2.3 %shard_map.193.held = bf16[16,64,128]{2,1,0:T(8,128)(2,1)S(1)} custom-call(s32[2,4]{1,0:T(2,128)S(1)} %copy-done.5, s32[2]{0:T(128)S(1)} %copy-done.6, f32[256,128]{1,0:T(8,128)S(1)} %copy-done.1, bf16[32,32]{1,0:T(8,128)(2,1)S(1)} %copy-done.4), custom_call_target="tpu_custom_call" | custom-call | flops 100000000 | bytes 1000000 | tf_op jit(solution)/shard_map/pallas_call | solution.py:411
  67.4 5.9 %all-to-all-done.2.got = f32[32,4,128]{2,1,0:T(4,128)S(1)} async-done(((f32[32,4,128]{2,1,0:T(4,128)}), f32[32,4,128]{2,1,0:T(4,128)S(1)}, u32[]{:S(2)}, u32[]{:S(2)}) %all-to-all-start.2) | async-done | bytes 65568 | tf_op jit(solution)/shard_map/all_to_all | solution.py:430
  73.3 1.2 %shard_map.194 = bf16[16,96,128]{2,1,0:T(8,128)(2,1)} custom-call(f32[32,4,128]{2,1,0:T(4,128)S(1)} %all-to-all-done.2.got, f32[128,64]{1,0:T(8,128)S(1)} %copy-done, bf16[16,64,128]{2,1,0:T(8,128)(2,1)S(1)} %shard_map.193.held), custom_call_target="tpu_custom_call" | custom-call | flops 100000000 | bytes 500000 | tf_op jit(solution)/shard_map/pallas_call | solution.py:431
  74.5 0.0 copy-start.3
  74.5 6.2 %all-to-all-start.3 = ((bf16[16,96,128]{2,1,0:T(8,128)(2,1)}), bf16[16,96,128]{2,1,0:T(8,128)(2,1)S(1)}, u32[]{:S(2)}, u32[]{:S(2)}) async-start(bf16[16,96,128]{2,1,0:T(8,128)(2,1)} %shard_map.194), calls=%async_computation.3 | async-start | bytes 786432 | tf_op jit(solution)/shard_map/all_to_all | solution.py:437
  80.7 0.0 copy-start.9
  80.7 0.6 copy-done.9
  81.4 0.1 copy.21.bias
  81.5 13.8 %all-to-all-done.3.got = bf16[16,96,128]{2,1,0:T(8,128)(2,1)S(1)} async-done(((bf16[16,96,128]{2,1,0:T(8,128)(2,1)}), bf16[16,96,128]{2,1,0:T(8,128)(2,1)S(1)}, u32[]{:S(2)}, u32[]{:S(2)}) %all-to-all-start.3) | async-done | bytes 393248 | tf_op jit(solution)/shard_map/all_to_all | solution.py:437
  95.3 0.0 copy-done.3
  95.3 2.1 %shard_map.195 = f32[4,8,32,128]{3,2,1,0:T(8,128)} custom-call(s32[8,128]{1,0:T(8,128)S(1)} %get-tuple-element.10.slots, bf16[16,96,128]{2,1,0:T(8,128)(2,1)S(1)} %all-to-all-done.3.got, bf16[64,256]{1,0:T(8,128)(2,1)S(1)} %copy-done.3, f32[32,1]{1,0:T(8,128)S(1)} %copy.21.bias), custom_call_target="tpu_custom_call" | custom-call | flops 100000000 | bytes 1000000 | tf_op jit(solution)/shard_map/pallas_call | solution.py:438
Async XLA Ops:
  0.0 49.7 %copy-start.8 = (bf16[32,1,2,2,32,32]{5,4,3,2,1,0:T(8,128)(2,1)S(1)}, bf16[32,1,2,2,32,32]{5,4,3,2,1,0:T(8,128)(2,1)}, u32[]{:S(2)}) copy-start(bf16[32,1,2,2,32,32]{5,4,3,2,1,0:T(8,128)(2,1)} %param.33) | copy-start | bytes 786436
  17.8 16.0 %copy-start.7 = (bf16[512,128]{1,0:T(8,128)(2,1)S(1)}, bf16[512,128]{1,0:T(8,128)(2,1)}, u32[]{:S(2)}) copy-start(bf16[512,128]{1,0:T(8,128)(2,1)} %constant.11.clone.phase) | copy-start | bytes 393220
  34.9 23.7 %all-to-all-start.1 = ((f32[32,4,128]{2,1,0:T(4,128)}), f32[32,4,128]{2,1,0:T(4,128)S(1)}, u32[]{:S(2)}, u32[]{:S(2)}) async-start(f32[32,4,128]{2,1,0:T(4,128)} %get-tuple-element.11), calls=%async_computation.1 | async-start | bytes 131072 | tf_op jit(solution)/shard_map/all_to_all | solution.py:423
  49.7 8.9 %copy-start = (f32[128,64]{1,0:T(8,128)S(1)}, f32[128,64]{1,0:T(8,128)}, u32[]{:S(2)}) copy-start(f32[128,64]{1,0:T(8,128)} %constant.13.clone.back) | copy-start | bytes 98308
  49.7 8.8 %copy-start.2 = (f32[32,256]{1,0:T(8,128)S(1)}, f32[32,256]{1,0:T(8,128)}, u32[]{:S(2)}) copy-start(f32[32,256]{1,0:T(8,128)} %constant.12.clone.forward) | copy-start | bytes 98308
  58.6 5.9 %copy-start.4 = (bf16[32,32]{1,0:T(8,128)(2,1)S(1)}, bf16[32,32]{1,0:T(8,128)(2,1)}, u32[]{:S(2)}) copy-start(bf16[32,32]{1,0:T(8,128)(2,1)} %wp.1) | copy-start | bytes 6148
  60.4 4.0 %copy-start.1 = (f32[256,128]{1,0:T(8,128)S(1)}, f32[256,128]{1,0:T(8,128)}, u32[]{:S(2)}) copy-start(f32[256,128]{1,0:T(8,128)} %get-tuple-element.12.sums) | copy-start | bytes 393220
  60.4 12.9 %all-to-all-start.2 = ((f32[32,4,128]{2,1,0:T(4,128)}), f32[32,4,128]{2,1,0:T(4,128)S(1)}, u32[]{:S(2)}, u32[]{:S(2)}) async-start(f32[32,4,128]{2,1,0:T(4,128)} %shard_map.192), calls=%async_computation.2 | async-start | bytes 131072 | tf_op jit(solution)/shard_map/all_to_all | solution.py:430
  64.4 0.7 copy-start.5
  64.4 0.7 copy-start.6
  74.5 20.8 %copy-start.3 = (bf16[64,256]{1,0:T(8,128)(2,1)S(1)}, bf16[64,256]{1,0:T(8,128)(2,1)}, u32[]{:S(2)}) copy-start(bf16[64,256]{1,0:T(8,128)(2,1)} %constant.14.clone.inverse) | copy-start | bytes 98308
  74.5 20.8 %all-to-all-start.3 = ((bf16[16,96,128]{2,1,0:T(8,128)(2,1)}), bf16[16,96,128]{2,1,0:T(8,128)(2,1)S(1)}, u32[]{:S(2)}, u32[]{:S(2)}) async-start(bf16[16,96,128]{2,1,0:T(8,128)(2,1)} %shard_map.194), calls=%async_computation.3 | async-start | bytes 786432 | tf_op jit(solution)/shard_map/all_to_all | solution.py:437
  80.7 0.7 copy-start.9

commit v2 on v1

--- a/solution.py
+++ b/solution.py
@@ -55,6 +55,13 @@
     return high, (x - high.astype(F32)).astype(BF16)
 
 
+def table_dot(table, x):
+    high, low = halves(x)
+    rows = table.shape[0] // 2
+    both = dot(table, high)
+    return both[:rows] + both[rows:] + dot(table[:rows], low)
+
+
 def sin_cos(x):
     count = jnp.floor(x * (2.0 / math.pi) + 0.5)
     rest = x - count * HALF_PI[0]
@@ -101,10 +108,10 @@
     along_y = angles(size_y, True)
     per_row = np.repeat(along_y.T, CX, axis=0)
     phase_y = np.concatenate(split_table(np.cos(per_row)) + split_table(np.sin(per_row)), 0)
-    back_y = f32(np.concatenate([np.cos(along_y), np.sin(along_y)], 1))
+    back_y = np.concatenate(split_table(np.concatenate([np.cos(along_y), np.sin(along_y)], 1)), 0)
     along_x = angles(size_x, True)
-    forward_x = f32(np.concatenate([np.cos(along_x), np.sin(along_x)], 0).T.reshape(MODES, 2 * size_x))
-    back_x = f32(np.concatenate([np.cos(along_x), np.sin(along_x)], 1))
+    forward_x = np.concatenate(split_table(np.concatenate([np.cos(along_x), np.sin(along_x)], 0).T), 0)
+    back_x = np.concatenate(split_table(np.concatenate([np.cos(along_x), np.sin(along_x)], 1)), 0)
     return forward_z, inverse_z, phase_y, back_y, forward_x, back_x
 
 
@@ -192,9 +199,8 @@
     held[...] = jnp.zeros_like(held)
     table = fz[...]
     for j in range(PAIRS):
-        high, low = by_cell[0][j], by_cell[1][j]
-        both = dot(table, high)
-        full = both[: 4 * N_GY] + both[4 * N_GY :] + dot(table[: 4 * N_GY], low)
+        both = dot(table, by_cell[0][j])
+        full = both[: 4 * N_GY] + both[4 * N_GY :] + dot(table[: 4 * N_GY], by_cell[1][j])
         picked = jnp.zeros((N_GY, 4 * C), F32)
         for g in range(4):
             picked = jnp.where(lane_group == g, full[g * N_GY : (g + 1) * N_GY], picked)
@@ -232,38 +238,53 @@
     return terms
 
 
-def map_kernel(owner, live, sums, wp, out):
-    high, low = spread_cells(sums[...])
-    eye = (iota((C, 4 * C), 0) == iota((C, 4 * C), 1)).astype(BF16)
-    wpt = dot(wp[...], eye, TN).astype(BF16)
-    out[...] = jnp.zeros_like(out)
-    for j in range(PAIRS):
-        b, s = divmod(j, LIST)
-        mapped = dot(wpt, high[j], NT) + dot(wpt, low[j], NT)
-
-        @pl.when(s < live[b])
-        def _(b=b, s=s, mapped=mapped):
-            out[owner[b, s], b * C : (b + 1) * C, :] = mapped.astype(out.dtype)
+def tile_kernel(slots, got, wp, bias, out, raw):
+    raw[...] = jnp.zeros_like(raw)
+    for n in range(N_GY * BLK):
+        v = slots[0, n]
+
+        @pl.when(v >= 0)
+        def _(n=n, v=v):
+            t = pl.multiple_of((v & (CX * CY - 1)) * (NZ // 4), NZ // 4)
+            at = pl.multiple_of((n * LIST + v // (CX * CY)) * (NZ // 4), NZ // 4)
+            raw[pl.ds(t, NZ // 4), :] = raw[pl.ds(t, NZ // 4), :] + got[pl.ds(at, NZ // 4), :]
+
+    pick = ((iota((4 * C, C), 0) & (C - 1)) == iota((4 * C, C), 1)).astype(BF16)
+    spread = dot(dot(pick, wp[...], NT).astype(BF16), pick, NT)
+    same = (iota(spread.shape, 0) // C) == (iota(spread.shape, 1) // C)
+    weights = jnp.where(same, spread, 0.0).astype(BF16)
+    column = jnp.broadcast_to(bias[...], (C, NZ))
+    group = iota((C, NZ), 1) // (NZ // 4)
+    for q in range(CX * CY // 4):
+        high, low = halves(raw[q * NZ : (q + 1) * NZ, :])
+        mapped = dot(weights, high, NT) + dot(weights, low, NT)
+        for t in range(4):
+            line = jnp.zeros((C, NZ), F32)
+            for k in range(4):
+                piece = mapped[k * C : (k + 1) * C]
+                shift = ((k - t) * (NZ // 4)) % NZ
+                line = jnp.where(group == k, piece if shift == 0 else pltpu.roll(piece, shift, 1), line)
+            out[q * 4 + t] = line + column
 
 
 def y_kernel(got, phase, out, slots):
     gy = lax.axis_index("gy")
     full = got[...].astype(F32)
     values = full[:, :PAIRS, :].reshape(N_GY * PAIRS, 128)
-    extra = full[:, PAIRS:, :]
-    sent = jnp.sum(extra, axis=0)
+    sent = jnp.sum(full[:, PAIRS:, :], axis=0)
     xs, ys, on = sent[0:1], sent[1:2], sent[2:3]
     square = (128, 128)
     hot = ((iota(square, 0).astype(F32) == ys) & (on > 0.5)).astype(BF16)
     turned = dot(phase[...], hot)
-    here = (iota(square, 0) & (CX - 1)).astype(F32) == xs
-    cosine = jnp.where(here, turned[0:128] + turned[128:256], 0.0)
-    sine = jnp.where(here, turned[256:384] + turned[384:512], 0.0)
-    result = fine_dot(cosine, values) + fine_dot(sine, rotated(values, 1.0))
+    here = (iota((512, 128), 0) & (CX - 1)).astype(F32) == xs
+    turned = jnp.where(here, turned, 0.0).astype(BF16)
+    both = dot(turned[:256], values.astype(BF16)) + dot(turned[256:], rotated(values, 1.0).astype(BF16))
+    result = both[:128] + both[128:]
     out[...] = result.reshape(MODES, CX, 128).astype(out.dtype)
     yi = ys.astype(jnp.int32)
     mine = ((yi // CY) == gy) & (on > 0.5)
-    number = jnp.where(mine, xs.astype(jnp.int32) * CY + (yi & (CY - 1)) + 1, 0).astype(BF16)
+    number = xs.astype(jnp.int32) * CY + (yi & (CY - 1)) + (iota((1, 128), 1) & (LIST - 1)) * (CX * CY) + 1
+    number = jnp.where(mine, number, 0).astype(BF16)
     group = ((iota(square, 0) // LIST) == iota(square, 1)).astype(BF16)
     slots[...] = dot(jnp.broadcast_to(number, (8, 128)), group).astype(jnp.int32) - 1
 
@@ -278,7 +299,7 @@
 def x_kernel(got, weights, forward, back, out):
     size_x = CX * N_GX
     values = got[...].astype(F32).reshape(size_x, 128)
-    spectrum = fine_dot(forward[:, :size_x], values) + fine_dot(forward[:, size_x:], rotated(values, 1.0))
+    spectrum = table_dot(forward[...], jnp.concatenate([values, rotated(values, 1.0)], axis=0))
     parts = [spectrum if g == 0 else pltpu.roll(spectrum, 128 - g * C, 1) for g in range(4)]
     high, low = halves(jnp.concatenate(parts, axis=0))
     spread = ((iota((128, C * C), 1) // C) == iota((128, C * C), 0)).astype(BF16)
@@ -303,12 +324,11 @@
     r0, i0, r1, i1 = totals
     mixed = jnp.where(group == 0, r0, jnp.where(group == 1, i0, jnp.where(group == 2, r1, i1)))
     other = jnp.where(group == 0, -i0, jnp.where(group == 1, r0, jnp.where(group == 2, -i1, r1)))
-    result = fine_dot(back[...], jnp.concatenate([mixed, other], axis=0))
+    result = table_dot(back[...], jnp.concatenate([mixed, other], axis=0))
     out[...] = result.reshape(N_GX, CX, 128).astype(out.dtype)
 
 
-def back_kernel(got, back, held, out):
-    out[:, 4 * CY :, :] = held[...]
+def back_kernel(got, back, out):
     lines = [got[:, x, :].astype(F32) for x in range(CX)]
     group = iota((MODES, 128), 1) // C
     turned = []
@@ -319,41 +339,26 @@
             moved = lines[x] if shift == 0 else pltpu.roll(lines[x], shift, 1)
             line = jnp.where(group == x, moved, line)
         turned.append(line)
-    size_y = CY * N_GY
-    for k in range(2):
-        real, imag = turned[2 * k], turned[2 * k + 1]
-        stack = jnp.concatenate(
-            [jnp.concatenate([real, imag], axis=1), jnp.concatenate([-imag, real], axis=1)], axis=0
-        )
-        result = fine_dot(back[...], stack)
-        for g in range(2):
-            piece = result[:, g * 128 : (g + 1) * 128].reshape(N_GY, CY, 128)
-            at = (2 * k + g) * CY
-            out[:, at : at + CY, :] = piece.astype(out.dtype)
-
-
-def end_kernel(slots, got, inverse, bias, out, wide, total):
-    wide[...] = got[:, : 4 * CY, :].astype(F32).reshape(N_GY * 4 * CY, 128)
-    column = jnp.broadcast_to(bias[...], (C, NZ))
+    r0, i0, r1, i1 = turned
+    stack = jnp.concatenate(
+        [jnp.concatenate(turned, axis=1), jnp.concatenate([-i0, r0, -i1, r1], axis=1)], axis=0
+    )
+    result = table_dot(back[...], stack)
+    for g in range(4):
+        piece = result[:, g * 128 : (g + 1) * 128].reshape(N_GY, CY, 128)
+        out[:, g * CY : (g + 1) * CY, :] = piece.astype(out.dtype)
+
+
+def end_kernel(got, inverse, known, out, wide):
+    wide[...] = got[...].astype(F32).reshape(N_GY * 4 * CY, 128)
     for y in range(CY):
         values = wide[pl.ds(y, 4 * N_GY, stride=CY), :].astype(BF16)
         both = dot(values, inverse[...], TN)
         line = both[:, :NZ] + both[:, NZ:]
         for x in range(CX):
-            total[x * CY + y] = line[x * C : (x + 1) * C] + column
-    for n in range(N_GY * BLK):
-        src, b = divmod(n, BLK)
-        t = slots[0, n]
-
-        @pl.when(t >= 0)
-        def _(src=src, b=b, t=t):
-            at = 4 * CY + b * C
-            total[t] = total[t] + got[src, at : at + C, :].astype(F32)
-
-    for t in range(CX * CY):
-        h = total[t]
-        th = jnp.tanh(h * (GELU_B * (h * h) + GELU_A))
-        out[t // CY, t % CY] = 0.5 * (h + h * th)
+            h = line[x * C : (x + 1) * C] + known[x * CY + y]
+            th = jnp.tanh(h * (GELU_B * (h * h) + GELU_A))
+            out[x, y] = 0.5 * (h + h * th)
 
 
 def call(kernel, out_shape, in_specs, scratch=(), flops=0, size=0, vmem=40 * 1024 * 1024):
@@ -408,12 +413,7 @@
         w_first, b_first, w_second, b_second, w_third,
     )
     modes = lax.all_to_all(modes, "gy", 0, 0, tiled=True)
-    mapped = call(
-        map_kernel,
-        jax.ShapeDtypeStruct((N_GY, BLK * C, NZ), BF16),
-        [SM, SM] + [VM] * 2,
-        flops=100_000_000, size=1_000_000,
-    )(tile_owner, live_count, sums, w_point)
+    sums = lax.all_gather(sums, "gy", axis=0, tiled=True)
     along_y, slots = call(
         y_kernel,
         (jax.ShapeDtypeStruct((MODES, CX, 128), F32), jax.ShapeDtypeStruct((8, 128), jnp.int32)),
@@ -430,18 +430,25 @@
     lines = lax.all_to_all(lines, "gx", 0, 0, tiled=True)
     cells = call(
         back_kernel,
-        jax.ShapeDtypeStruct((N_GY, 4 * CY + BLK * C, NZ), BF16),
-        [VM] * 3,
+        jax.ShapeDtypeStruct((N_GY, 4 * CY, 128), BF16),
+        [VM] * 2,
         flops=100_000_000, size=500_000,
-    )(lines, back_y, mapped)
+    )(lines, back_y)
+    known = call(
+        tile_kernel,
+        jax.ShapeDtypeStruct((CX * CY, C, NZ), F32),
+        [SM] + [VM] * 3,
+        [vm((CX * CY * NZ // 4, 4 * C), F32)],
+        flops=100_000_000, size=2_500_000,
+    )(slots, sums, w_point, b_point.reshape(C, 1))
     cells = lax.all_to_all(cells, "gy", 0, 0, tiled=True)
     return call(
         end_kernel,
         jax.ShapeDtypeStruct((CX, CY, C, NZ), F32),
-        [SM] + [VM] * 3,
-        [vm((N_GY * 4 * CY, 128), F32), vm((CX * CY, C, NZ), F32)],
+        [VM] * 3,
+        [vm((N_GY * 4 * CY, 128), F32)],
         flops=100_000_000, size=1_000_000,
-    )(slots, cells, inverse_z, b_point.reshape(C, 1))
+    )(cells, inverse_z, known)
 
 
 def solution(mesh):

time: 97.9 us -> 104 us (1.062)
  blocking collectives: 16 us -> 30.1 us
  waiting for transfers between devices: 27.4 us -> 13.4 us
  between operations: 0.1 us -> 13.5 us
  Pallas kernels: 26.4 us -> 21.6 us
  starting transfers between devices: 25 us -> 21.7 us
    all_to_all x0 -> x1, blocking collectives: none -> 12 us  [local(): lines = lax.all_to_all(lines, 'gx', 0, 0, tiled=True)]
    all_to_all x1, waiting for transfers between devices: 13.8 us -> 5.61 us  [local(): cells = lax.all_to_all(cells, 'gy', 0, 0, tiled=True)]
    all_to_all x1 -> x0, waiting for transfers between devices: 5.91 us -> none  [local(): lines = lax.all_to_all(lines, 'gx', 0, 0, tiled=True)]
    all_to_all x1 -> x0, starting transfers between devices: 3.99 us -> none  [local(): lines = lax.all_to_all(lines, 'gx', 0, 0, tiled=True)]
    pallas_call x1, Pallas kernels: 17.8 us -> 15.6 us  [stage_one(): call(pair_kernel, (jax.ShapeDtypeStruct((N_GY, 16, 128), BF16), jax.Shape...]
    all_to_all x1, blocking collectives: 16 us -> 18.1 us  [local(): modes = lax.all_to_all(modes, 'gy', 0, 0, tiled=True)]
    pallas_call x3, Pallas kernels: 5.62 us -> 4.11 us  [the longest x1 1.9 us: local(): call(tile_kernel, jax.ShapeDtypeStruct((CX * CY, C, NZ), F32), [SM] + [VM...]
  transfers between devices with their start and end apart: 3 -> 3, of which waited for: 3 -> 2; matrix products, arithmetic and copies ran while one was open for 1% -> 1% of each run, Pallas kernels for 2% -> 5%
where the time goes in v2:
time: 104 us; the launch traced here: 103 us
  blocking collectives  30.1 us (29%)
  starting transfers between devices  21.7 us (21%)
  Pallas kernels  21.6 us (21%)
  between operations  13.5 us (13%)
  waiting for transfers between devices  13.4 us (13%)
  local copies, waits for them, and re-layouts  2.82 us (3%)
    all_to_all x1, blocking collectives, local(): modes = lax.all_to_all(modes, 'gy', 0, 0, tiled=True)  18.1 us
    all_to_all x1, starting transfers between devices, local(): along_y = lax.all_to_all(along_y, 'gx', 0, 0, tiled=True)  15.7 us
    pallas_call x1, Pallas kernels, stage_one(): call(pair_kernel, (jax.ShapeDtypeStruct((N_GY, 16, 128), BF16), jax.Shape...  15.6 us
    all_to_all x1, blocking collectives, local(): lines = lax.all_to_all(lines, 'gx', 0, 0, tiled=True)  12 us
    all_to_all x1, waiting for transfers between devices, local(): along_y = lax.all_to_all(along_y, 'gx', 0, 0, tiled=True)  7.72 us
    all_to_all x1, starting transfers between devices, local(): cells = lax.all_to_all(cells, 'gy', 0, 0, tiled=True)  6.04 us
    all_to_all x1, waiting for transfers between devices, local(): cells = lax.all_to_all(cells, 'gy', 0, 0, tiled=True)  5.61 us
  transfers between devices with their start and end apart: 3, of which 2 were waited for; matrix products, arithmetic and copies ran while one was open for 1% of the time, Pallas kernels for 5%

profile of v2, /device:TPU:1, one launch (start us, length us, event | category | flops | bytes accessed | tf_op | source)
XLA Modules:
  0.0 103.1 jit_solution(15458094299117569122)
XLA Ops:
  6.5 0.0 all-gather.2.cloned.1.call-start
  6.5 0.0 copy-start.5
  6.5 0.0 copy-start.6
  6.5 15.6 %shard_map.190 = (bf16[16,16,128]{2,1,0:T(8,128)(2,1)}, f32[256,128]{1,0:T(8,128)}) custom-call(s32[2,4]{1,0:T(2,128)} %owner.1, s32[2,4]{1,0:T(2,128)} %tile.1, s32[2]{0:T(128)} %live.1, bf16[32,256]{1,0:T(8,128)(2,1)} %feats.1, bf16[3,256]{1,0:T(4,128)(2,1)} %offs.1, s32[1,256]{1,0:T(1,128)} %bitcast.8, bf16[3,64]{1,0:T(4,128)(2,1)} %bitcast.9, ...), custom_call_target="tpu_custom_call" | custom-call | flops 1600000000 | bytes 1000000 | tf_op jit(solution)/shard_map/pallas_call | solution.py:385
  22.2 0.0 copy-start.1
  22.2 0.0 copy-start.3
  22.2 0.0 copy-start.7
  22.2 0.0 copy-start.4
  22.2 0.0 all-gather.2.cloned.1.call-update
  22.2 18.1 %all_to_all.20.got = bf16[16,16,128]{2,1,0:T(8,128)(2,1)S(1)} all-to-all(bf16[16,16,128]{2,1,0:T(8,128)(2,1)} %get-tuple-element.9), channel_id=1, replica_groups=mesh['gx'=32,'gy'=16] {'gy'}, dimensions={0} | all-to-all | bytes 131072 | tf_op jit(solution)/shard_map/all_to_all | solution.py:415
  40.3 0.0 copy-done.5
  40.3 1.0 shard_map.191
  41.3 15.7 %all-to-all-start.1 = ((f32[32,4,128]{2,1,0:T(4,128)}), f32[32,4,128]{2,1,0:T(4,128)S(1)}, u32[]{:S(2)}, u32[]{:S(2)}) async-start(f32[32,4,128]{2,1,0:T(4,128)} %get-tuple-element.10), calls=%async_computation.1 | async-start | bytes 131072 | tf_op jit(solution)/shard_map/all_to_all | solution.py:423
  57.0 0.0 copy-done.6
  57.0 1.1 %reshape.18.weights = bf16[32,4096]{1,0:T(8,128)(2,1)S(1)} reshape(bf16[32,1,2,2,32,32]{5,4,3,2,1,0:T(8,128)(2,1)S(1)} %copy-done.6) | data formatting | bytes 524288 | tf_op jit(solution)/shard_map/reshape | solution.py:429
  58.1 0.0 copy-start.2
  58.1 7.7 %all-to-all-done.1.got = f32[32,4,128]{2,1,0:T(4,128)S(1)} async-done(((f32[32,4,128]{2,1,0:T(4,128)}), f32[32,4,128]{2,1,0:T(4,128)S(1)}, u32[]{:S(2)}, u32[]{:S(2)}) %all-to-all-start.1) | async-done | bytes 65568 | tf_op jit(solution)/shard_map/all_to_all | solution.py:423
  65.9 0.0 copy-done.1
  65.9 0.0 copy-done.3
  65.9 0.9 shard_map.192
  66.8 12.0 %all_to_all.21.got = f32[32,4,128]{2,1,0:T(4,128)S(1)} all-to-all(f32[32,4,128]{2,1,0:T(4,128)S(1)} %shard_map.192), channel_id=1, replica_groups=mesh['gx'=32,'gy'=16] {'gx'}, dimensions={0} | all-to-all | bytes 131072 | tf_op jit(solution)/shard_map/all_to_all | solution.py:430
  78.8 1.0 shard_map.193
  79.8 6.0 %all-to-all-start.3 = ((bf16[16,32,128]{2,1,0:T(8,128)(2,1)}), bf16[16,32,128]{2,1,0:T(8,128)(2,1)S(1)}, u32[]{:S(2)}, u32[]{:S(2)}) async-start(bf16[16,32,128]{2,1,0:T(8,128)(2,1)} %shard_map.193), calls=%async_computation.3 | async-start | bytes 262144 | tf_op jit(solution)/shard_map/all_to_all | solution.py:444
  85.9 0.0 copy-done.7
  85.9 0.1 copy.21.bias
  85.9 0.0 all-gather.2.cloned.1.call-done.got
  86.0 0.0 copy-done.4
  86.0 0.0 copy-start
  86.0 1.6 %copy-done = f32[4096,128]{1,0:T(8,128)S(1)} copy-done((f32[4096,128]{1,0:T(8,128)S(1)}, f32[4096,128]{1,0:T(8,128)}, u32[]{:S(2)}) %copy-start) | copy-done | bytes 2097176
  87.5 1.9 %shard_map.194.known = f32[32,32,128]{2,1,0:T(8,128)S(1)} custom-call(s32[8,128]{1,0:T(8,128)S(1)} %get-tuple-element.11.slots, f32[4096,128]{1,0:T(8,128)S(1)} %copy-done, bf16[32,32]{1,0:T(8,128)(2,1)S(1)} %copy-done.4, f32[32,1]{1,0:T(8,128)S(1)} %copy.21.bias), custom_call_target="tpu_custom_call" | custom-call | flops 100000000 | bytes 2500000 | tf_op jit(solution)/shard_map/pallas_call | solution.py:437
  89.5 5.6 %all-to-all-done.3.got = bf16[16,32,128]{2,1,0:T(8,128)(2,1)S(1)} async-done(((bf16[16,32,128]{2,1,0:T(8,128)(2,1)}), bf16[16,32,128]{2,1,0:T(8,128)(2,1)S(1)}, u32[]{:S(2)}, u32[]{:S(2)}) %all-to-all-start.3) | async-done | bytes 131104 | tf_op jit(solution)/shard_map/all_to_all | solution.py:444
  95.1 0.0 copy-done.2
  95.1 1.2 %shard_map.195 = f32[4,8,32,128]{3,2,1,0:T(8,128)} custom-call(bf16[16,32,128]{2,1,0:T(8,128)(2,1)S(1)} %all-to-all-done.3.got, bf16[64,256]{1,0:T(8,128)(2,1)S(1)} %copy-done.2, f32[32,32,128]{2,1,0:T(8,128)S(1)} %shard_map.194.known), custom_call_target="tpu_custom_call" | custom-call | flops 100000000 | bytes 1000000 | tf_op jit(solution)/shard_map/pallas_call | solution.py:445
Async XLA Ops:
  6.5 79.4 %all-gather.2.cloned.1.call-start = ((), (), s32[]{:S(2)}) async-start(), calls=%async_computation.4 | async-start | bytes 2228224 | tf_op jit(solution)/shard_map/all_gather | solution.py:416
  6.5 33.8 %copy-start.5 = (bf16[512,128]{1,0:T(8,128)(2,1)S(1)}, bf16[512,128]{1,0:T(8,128)(2,1)}, u32[]{:S(2)}) copy-start(bf16[512,128]{1,0:T(8,128)(2,1)} %constant.11.clone.phase) | copy-start | bytes 393220
  6.5 50.5 %copy-start.6 = (bf16[32,1,2,2,32,32]{5,4,3,2,1,0:T(8,128)(2,1)S(1)}, bf16[32,1,2,2,32,32]{5,4,3,2,1,0:T(8,128)(2,1)}, u32[]{:S(2)}) copy-start(bf16[32,1,2,2,32,32]{5,4,3,2,1,0:T(8,128)(2,1)} %param.33) | copy-start | bytes 786436
  22.2 43.7 %copy-start.1 = (bf16[256,64]{1,0:T(8,128)(2,1)S(1)}, bf16[256,64]{1,0:T(8,128)(2,1)}, u32[]{:S(2)}) copy-start(bf16[256,64]{1,0:T(8,128)(2,1)} %constant.13.clone.back) | copy-start | bytes 98308
  22.2 43.7 %copy-start.3 = (bf16[64,256]{1,0:T(8,128)(2,1)S(1)}, bf16[64,256]{1,0:T(8,128)(2,1)}, u32[]{:S(2)}) copy-start(bf16[64,256]{1,0:T(8,128)(2,1)} %constant.12.clone.forward) | copy-start | bytes 98308
  22.2 63.7 %copy-start.7 = (f32[32]{0:T(128)S(1)}, f32[32]{0:T(128)}, u32[]{:S(2)}) copy-start(f32[32]{0:T(128)} %param.32) | copy-start | bytes 388
  22.2 63.8 %copy-start.4 = (bf16[32,32]{1,0:T(8,128)(2,1)S(1)}, bf16[32,32]{1,0:T(8,128)(2,1)}, u32[]{:S(2)}) copy-start(bf16[32,32]{1,0:T(8,128)(2,1)} %wp.1) | copy-start | bytes 6148
  41.3 24.5 %all-to-all-start.1 = ((f32[32,4,128]{2,1,0:T(4,128)}), f32[32,4,128]{2,1,0:T(4,128)S(1)}, u32[]{:S(2)}, u32[]{:S(2)}) async-start(f32[32,4,128]{2,1,0:T(4,128)} %get-tuple-element.10), calls=%async_computation.1 | async-start | bytes 131072 | tf_op jit(solution)/shard_map/all_to_all | solution.py:423
  58.1 36.9 %copy-start.2 = (bf16[64,256]{1,0:T(8,128)(2,1)S(1)}, bf16[64,256]{1,0:T(8,128)(2,1)}, u32[]{:S(2)}) copy-start(bf16[64,256]{1,0:T(8,128)(2,1)} %constant.14.clone.inverse) | copy-start | bytes 98308
  79.8 15.2 %all-to-all-start.3 = ((bf16[16,32,128]{2,1,0:T(8,128)(2,1)}), bf16[16,32,128]{2,1,0:T(8,128)(2,1)S(1)}, u32[]{:S(2)}, u32[]{:S(2)}) async-start(bf16[16,32,128]{2,1,0:T(8,128)(2,1)} %shard_map.193), calls=%async_computation.3 | async-start | bytes 262144 | tf_op jit(solution)/shard_map/all_to_all | solution.py:444
  86.0 1.6 %copy-start = (f32[4096,128]{1,0:T(8,128)S(1)}, f32[4096,128]{1,0:T(8,128)}, u32[]{:S(2)}) copy-start(f32[4096,128]{1,0:T(8,128)} %all-gather.2.cloned.1.call-done.got) | copy-start | bytes 6291460
Sparse Core Ops, SparseCore 0:
  22.3 52.1 all-gather.1

commit v3 on v2

--- a/solution.py
+++ b/solution.py
@@ -22,8 +22,7 @@
 LIST = 4
 PAIRS = BLK * LIST
 MODES = 32
-UNROLL = 1
-STACK = 32
+ANCHOR = 16
 VMEM_ONE = 62 * 1024 * 1024
 F32 = jnp.float32
 BF16 = jnp.bfloat16
@@ -117,19 +116,19 @@
 
 def pair_kernel(
     owner, tile, live, feats, offs, cells, w1, b1, b2, w2, w3, fz,
-    modes_out, sums,
-    cz, sz, w2b, w3b, side, point, feat, sin_p, cos_p, held,
+    sent,
+    sums, cz, sz, w2b, w3b, side, point, feat, sin_p, cos_p, held,
 ):
     gx = lax.axis_index("gx")
     gy = lax.axis_index("gy")
     pick = ((iota((4 * HID, HID), 0) & (HID - 1)) == iota((4 * HID, HID), 1)).astype(BF16)
     spread = dot(dot(pick, w2[...], NT).astype(BF16), pick, NT)
     same = (iota(spread.shape, 0) // HID) == (iota(spread.shape, 1) // HID)
-    w2b[...] = jnp.where(same, spread, 0.0).astype(BF16)
+    w2b[...] = jnp.where(same, spread, 0.0)
     pick_c = ((iota((4 * C, C), 0) & (C - 1)) == iota((4 * C, C), 1)).astype(BF16)
     spread = dot(dot(pick, w3[...], NT).astype(BF16), pick_c, NT)
     same = (iota(spread.shape, 0) // HID) == (iota(spread.shape, 1) // C)
-    w3b[...] = jnp.where(same, 0.5 * spread, 0.0).astype(BF16)
+    w3b[...] = jnp.where(same, 0.5 * spread, 0.0)
     shape = (HID, 4 * HID)
     pick_t = (iota(shape, 0) == (iota(shape, 1) & (HID - 1))).astype(F32)
     side[0:3, :] = fine_dot(w1[...].astype(F32), pick_t)
@@ -139,6 +138,7 @@
     sine, cosine = sin_cos(side[2:3, :] * cell_z)
     cz[...] = cosine
     sz[...] = sine
+    side[5:6, :] = 2.0 * sin_cos(jnp.broadcast_to(side[2:3, :], (8, 4 * HID)))[1][0:1]
     sums[...] = jnp.zeros_like(sums)
     row_of = iota((PB, PB), 0)
     for b in range(BLK):
@@ -166,31 +166,28 @@
             sine, cosine = sin_cos(line - point[b])
             sin_p[...] = sine
             cos_p[...] = cosine
-
-            def some_cells(i, carry):
-                for u in range(UNROLL):
-                    g = (i * UNROLL + u) * STACK
+            twice = side[5:6, :PB]
+
+            lines = []
+            for g in range(NZ // 4):
+                if g % ANCHOR < 2:
                     sp = sin_p[...]
                     cp = cos_p[...]
-                    lines = []
-                    for k in range(STACK):
-                        c = cz[pl.ds(g + k, 1), :]
-                        d = sz[pl.ds(g + k, 1), :]
-                        lines.append(
-                            jnp.concatenate(
-                                [sp * c[:, :PB] + cp * d[:, :PB], sp * c[:, PB:] + cp * d[:, PB:]], axis=1
-                            ).astype(BF16)
-                        )
-                    h = dot(jnp.concatenate(lines, axis=0), w2b[...]) + side[4:5, :]
-                    th = jnp.tanh(h * (GELU_B * (h * h) + GELU_A))
-                    second = (h + h * th).astype(BF16)
-                    kern = dot(second, w3b[...])
-                    for k in range(STACK):
-                        total = jnp.sum(kern[k * PB : (k + 1) * PB] * feat[b], axis=0, keepdims=True)
-                        sums[pl.ds((b * LIST + s) * (NZ // 4) + g + k, 1), :] = total
-                return carry
-
-            lax.fori_loop(0, NZ // 4 // (UNROLL * STACK), some_cells, 0)
+                    c = cz[g : g + 1, :]
+                    d = sz[g : g + 1, :]
+                    now = sp * c[:, :PB] + cp * d[:, :PB], sp * c[:, PB:] + cp * d[:, PB:]
+                else:
+                    now = twice * last[0] - before[0], twice * last[1] - before[1]
+                if g % ANCHOR:
+                    before = last
+                last = now
+                lines.append(jnp.concatenate(now, axis=1))
+            h = dot(jnp.concatenate(lines, axis=0), w2b[...]) + side[4:5, :]
+            th = jnp.tanh(h * (GELU_B * (h * h) + GELU_A))
+            kern = dot(h + h * th, w3b[...])
+            for g in range(NZ // 4):
+                total = jnp.sum(kern[g * PB : (g + 1) * PB] * feat[b], axis=0, keepdims=True)
+                sums[pl.ds((b * LIST + s) * (NZ // 4) + g, 1), :] = total
             return carry
 
         lax.fori_loop(0, live[b], one_pair, 0)
@@ -218,7 +215,16 @@
         on = jnp.where(here & (s < live[b]), 1, on)
     for k, v in enumerate((xs, ys, on)):
         held[:, PAIRS + k, :] = jnp.broadcast_to(v.astype(F32), (N_GY, 128))
-    modes_out[...] = held[...].astype(modes_out.dtype)
+    sent[:, :16, :] = held[...].astype(sent.dtype)
+    sent[:, 16:, :] = jnp.zeros((N_GY, BLK * NZ // 4, 4 * C), sent.dtype)
+    for j in range(PAIRS):
+        b, s = divmod(j, LIST)
+
+        @pl.when(s < live[b])
+        def _(b=b, s=s, j=j):
+            at = 16 + b * (NZ // 4)
+            rows = sums[j * (NZ // 4) : (j + 1) * (NZ // 4), :]
+            sent[owner[b, s], at : at + NZ // 4, :] = rows.astype(sent.dtype)
 
 
 def spread_cells(sums):
@@ -241,13 +247,14 @@
 def tile_kernel(slots, got, wp, bias, out, raw):
     raw[...] = jnp.zeros_like(raw)
     for n in range(N_GY * BLK):
+        src, b = divmod(n, BLK)
         v = slots[0, n]
 
         @pl.when(v >= 0)
-        def _(n=n, v=v):
-            t = pl.multiple_of((v & (CX * CY - 1)) * (NZ // 4), NZ // 4)
-            at = pl.multiple_of((n * LIST + v // (CX * CY)) * (NZ // 4), NZ // 4)
-            raw[pl.ds(t, NZ // 4), :] = raw[pl.ds(t, NZ // 4), :] + got[pl.ds(at, NZ // 4), :]
+        def _(src=src, b=b, v=v):
+            t = pl.multiple_of(v * (NZ // 4), NZ // 4)
+            at = 16 + b * (NZ // 4)
+            raw[pl.ds(t, NZ // 4), :] = raw[pl.ds(t, NZ // 4), :] + got[src, at : at + NZ // 4, :].astype(F32)
 
     pick = ((iota((4 * C, C), 0) & (C - 1)) == iota((4 * C, C), 1)).astype(BF16)
     spread = dot(dot(pick, wp[...], NT).astype(BF16), pick, NT)
@@ -269,7 +276,7 @@
 
 def y_kernel(got, phase, out, slots):
     gy = lax.axis_index("gy")
-    full = got[...].astype(F32)
+    full = got[:, :16, :].astype(F32)
     values = full[:, :PAIRS, :].reshape(N_GY * PAIRS, 128)
     sent = jnp.sum(full[:, PAIRS:, :], axis=0)
     xs, ys, on = sent[0:1], sent[1:2], sent[2:3]
@@ -283,8 +290,7 @@
     out[...] = result.reshape(MODES, CX, 128).astype(out.dtype)
     yi = ys.astype(jnp.int32)
     mine = ((yi // CY) == gy) & (on > 0.5)
-    number = xs.astype(jnp.int32) * CY + (yi & (CY - 1)) + (iota((1, 128), 1) & (LIST - 1)) * (CX * CY) + 1
-    number = jnp.where(mine, number, 0).astype(BF16)
+    number = jnp.where(mine, xs.astype(jnp.int32) * CY + (yi & (CY - 1)) + 1, 0).astype(BF16)
     group = ((iota(square, 0) // LIST) == iota(square, 1)).astype(BF16)
     slots[...] = dot(jnp.broadcast_to(number, (8, 128)), group).astype(jnp.int32) - 1
 
@@ -384,14 +390,12 @@
     vm = pltpu.VMEM
     return call(
         pair_kernel,
-        (
-            jax.ShapeDtypeStruct((N_GY, 16, 128), BF16),
-            jax.ShapeDtypeStruct((PAIRS * NZ // 4, 4 * C), F32),
-        ),
+        jax.ShapeDtypeStruct((N_GY, 16 + BLK * NZ // 4, 128), BF16),
         [SM, SM, SM] + [VM] * 9,
         [
+            vm((PAIRS * NZ // 4, 4 * C), F32),
             vm((NZ // 4, 4 * HID), F32), vm((NZ // 4, 4 * HID), F32),
-            vm((4 * HID, 4 * HID), BF16), vm((4 * HID, 4 * C), BF16),
+            vm((4 * HID, 4 * HID), F32), vm((4 * HID, 4 * C), F32),
             vm((8, 4 * HID), F32), vm((BLK, PB, PB), F32), vm((BLK, PB, PB), F32),
             vm((PB, PB), F32), vm((PB, PB), F32), vm((N_GY, 16, 128), F32),
         ],
@@ -408,18 +412,17 @@
 ):
     _, inverse_z, phase_y, back_y, forward_x, back_x = tables(CX * N_GX, CY * N_GY)
     vm = pltpu.VMEM
-    modes, sums = stage_one(
+    sent = stage_one(
         features, offsets, point_cell, tile_owner, tile_local, live_count,
         w_first, b_first, w_second, b_second, w_third,
     )
-    modes = lax.all_to_all(modes, "gy", 0, 0, tiled=True)
-    sums = lax.all_gather(sums, "gy", axis=0, tiled=True)
+    sent = lax.all_to_all(sent, "gy", 0, 0, tiled=True)
     along_y, slots = call(
         y_kernel,
         (jax.ShapeDtypeStruct((MODES, CX, 128), F32), jax.ShapeDtypeStruct((8, 128), jnp.int32)),
         [VM, VM],
         flops=100_000_000, size=500_000,
-    )(modes, phase_y)
+    )(sent, phase_y)
     along_y = lax.all_to_all(along_y, "gx", 0, 0, tiled=True)
     lines = call(
         x_kernel,
@@ -440,7 +443,7 @@
         [SM] + [VM] * 3,
         [vm((CX * CY * NZ // 4, 4 * C), F32)],
         flops=100_000_000, size=2_500_000,
-    )(slots, sums, w_point, b_point.reshape(C, 1))
+    )(slots, sent, w_point, b_point.reshape(C, 1))
     cells = lax.all_to_all(cells, "gy", 0, 0, tiled=True)
     return call(
         end_kernel,

time: 104 us -> 92.4 us (0.89)
  between operations: 13.5 us -> 0.07 us
  blocking collectives: 30.1 us -> 39.5 us
  starting transfers between devices: 21.7 us -> 18 us
  Pallas kernels: 21.6 us -> 18.1 us
    all_to_all x1, blocking collectives: 18.1 us -> 27.1 us  [local(): sent = lax.all_to_all(sent, 'gy', 0, 0, tiled=True)]
    pallas_call x1, Pallas kernels: 15.6 us -> 12.1 us  [stage_one(): call(pair_kernel, jax.ShapeDtypeStruct((N_GY, 16 + BLK * NZ // 4, 128), B...]
    all_to_all x1, starting transfers between devices: 15.7 us -> 12.6 us  [local(): along_y = lax.all_to_all(along_y, 'gx', 0, 0, tiled=True)]
  transfers between devices with their start and end apart: 3 -> 2, of which waited for: 2 -> 2; matrix products, arithmetic and copies ran while one was open for 1% -> 1% of each run, Pallas kernels for 5% -> 2%
where the time goes in v3:
time: 92.4 us; the launch traced here: 91.9 us
  blocking collectives  39.5 us (43%)
  Pallas kernels  18.1 us (20%)
  starting transfers between devices  18 us (19%)
  waiting for transfers between devices  13.8 us (15%)
  local copies, waits for them, and re-layouts  2.53 us (3%)
    all_to_all x1, blocking collectives, local(): sent = lax.all_to_all(sent, 'gy', 0, 0, tiled=True)  27.1 us
    all_to_all x1, starting transfers between devices, local(): along_y = lax.all_to_all(along_y, 'gx', 0, 0, tiled=True)  12.6 us
    all_to_all x1, blocking collectives, local(): lines = lax.all_to_all(lines, 'gx', 0, 0, tiled=True)  12.4 us
    pallas_call x1, Pallas kernels, stage_one(): call(pair_kernel, jax.ShapeDtypeStruct((N_GY, 16 + BLK * NZ // 4, 128), B...  12.1 us
    all_to_all x1, waiting for transfers between devices, local(): along_y = lax.all_to_all(along_y, 'gx', 0, 0, tiled=True)  7.74 us
    all_to_all x1, waiting for transfers between devices, local(): cells = lax.all_to_all(cells, 'gy', 0, 0, tiled=True)  6.01 us
    all_to_all x1, starting transfers between devices, local(): cells = lax.all_to_all(cells, 'gy', 0, 0, tiled=True)  5.4 us
  transfers between devices with their start and end apart: 2, of which 2 were waited for; matrix products, arithmetic and copies ran while one was open for 1% of the time, Pallas kernels for 2%

profile of v3, /device:TPU:1, one launch (start us, length us, event | category | flops | bytes accessed | tf_op | source)
XLA Modules:
  0.0 91.9 jit_solution(17396224072101120782)
XLA Ops:
  0.0 12.1 %shard_map.190 = bf16[16,80,128]{2,1,0:T(8,128)(2,1)} custom-call(s32[2,4]{1,0:T(2,128)} %owner.1, s32[2,4]{1,0:T(2,128)} %tile.1, s32[2]{0:T(128)} %live.1, bf16[32,256]{1,0:T(8,128)(2,1)} %feats.1, bf16[3,256]{1,0:T(4,128)(2,1)} %offs.1, s32[1,256]{1,0:T(1,128)} %bitcast.8, bf16[3,64]{1,0:T(4,128)(2,1)} %bitcast.9, f32[1,64]{1,0:T(1,128)} %bitcast.10, ...), custom_call_target="tpu_custom_call" | custom-call | flops 1600000000 | bytes 1000000 | tf_op jit(solution)/shard_map/pallas_call | solution.py:391
  12.1 0.0 copy-start
  12.1 0.0 copy-start.5
  12.1 27.1 %all_to_all.20.got = bf16[16,80,128]{2,1,0:T(8,128)(2,1)S(1)} all-to-all(bf16[16,80,128]{2,1,0:T(8,128)(2,1)} %shard_map.190), channel_id=1, replica_groups=mesh['gx'=32,'gy'=16] {'gy'}, dimensions={0} | all-to-all | bytes 655360 | tf_op jit(solution)/shard_map/all_to_all | solution.py:419
  39.2 0.0 copy-done
  39.2 1.0 %shard_map.191 = (f32[32,4,128]{2,1,0:T(4,128)}, s32[8,128]{1,0:T(8,128)S(1)}) custom-call(bf16[16,80,128]{2,1,0:T(8,128)(2,1)S(1)} %all_to_all.20.got, bf16[512,128]{1,0:T(8,128)(2,1)S(1)} %copy-done), custom_call_target="tpu_custom_call" | custom-call | flops 100000000 | bytes 500000 | tf_op jit(solution)/shard_map/pallas_call | solution.py:420
  40.2 12.6 %all-to-all-start.1 = ((f32[32,4,128]{2,1,0:T(4,128)}), f32[32,4,128]{2,1,0:T(4,128)S(1)}, u32[]{:S(2)}, u32[]{:S(2)}) async-start(f32[32,4,128]{2,1,0:T(4,128)} %get-tuple-element.7), calls=%async_computation.1 | async-start | bytes 131072 | tf_op jit(solution)/shard_map/all_to_all | solution.py:426
  52.8 0.0 copy-done.5
  52.8 0.0 copy-start.1
  52.8 0.0 copy-start.3
  52.9 1.2 %reshape.18.weights = bf16[32,4096]{1,0:T(8,128)(2,1)S(1)} reshape(bf16[32,1,2,2,32,32]{5,4,3,2,1,0:T(8,128)(2,1)S(1)} %copy-done.5) | data formatting | bytes 524288 | tf_op jit(solution)/shard_map/reshape | solution.py:432
  54.0 7.7 %all-to-all-done.1.got = f32[32,4,128]{2,1,0:T(4,128)S(1)} async-done(((f32[32,4,128]{2,1,0:T(4,128)}), f32[32,4,128]{2,1,0:T(4,128)S(1)}, u32[]{:S(2)}, u32[]{:S(2)}) %all-to-all-start.1) | async-done | bytes 65568 | tf_op jit(solution)/shard_map/all_to_all | solution.py:426
  61.8 0.0 copy-done.1
  61.8 0.0 copy-done.3
  61.8 0.9 shard_map.192
  62.7 12.4 %all_to_all.21.got = f32[32,4,128]{2,1,0:T(4,128)S(1)} all-to-all(f32[32,4,128]{2,1,0:T(4,128)S(1)} %shard_map.192), channel_id=1, replica_groups=mesh['gx'=32,'gy'=16] {'gx'}, dimensions={0} | all-to-all | bytes 131072 | tf_op jit(solution)/shard_map/all_to_all | solution.py:433
  75.1 1.0 %shard_map.193 = bf16[16,32,128]{2,1,0:T(8,128)(2,1)} custom-call(f32[32,4,128]{2,1,0:T(4,128)S(1)} %all_to_all.21.got, bf16[256,64]{1,0:T(8,128)(2,1)S(1)} %copy-done.1), custom_call_target="tpu_custom_call" | custom-call | flops 100000000 | bytes 500000 | tf_op jit(solution)/shard_map/pallas_call | solution.py:434
  76.1 5.4 %all-to-all-start.3 = ((bf16[16,32,128]{2,1,0:T(8,128)(2,1)}), bf16[16,32,128]{2,1,0:T(8,128)(2,1)S(1)}, u32[]{:S(2)}, u32[]{:S(2)}) async-start(bf16[16,32,128]{2,1,0:T(8,128)(2,1)} %shard_map.193), calls=%async_computation.3 | async-start | bytes 262144 | tf_op jit(solution)/shard_map/all_to_all | solution.py:447
  81.5 0.0 copy-start.6
  81.5 0.6 copy-done.6
  82.1 0.0 copy-start.4
  82.1 0.1 copy.21.bias
  82.2 0.6 copy-done.4
  82.8 0.0 copy-start.2
  82.8 1.8 %shard_map.194.known = f32[32,32,128]{2,1,0:T(8,128)S(1)} custom-call(s32[8,128]{1,0:T(8,128)S(1)} %get-tuple-element.8.slots, bf16[16,80,128]{2,1,0:T(8,128)(2,1)S(1)} %all_to_all.20.got, bf16[32,32]{1,0:T(8,128)(2,1)S(1)} %copy-done.4, f32[32,1]{1,0:T(8,128)S(1)} %copy.21.bias), custom_call_target="tpu_custom_call" | custom-call | flops 100000000 | bytes 2500000 | tf_op jit(solution)/shard_map/pallas_call | solution.py:440
  84.7 6.0 %all-to-all-done.3.got = bf16[16,32,128]{2,1,0:T(8,128)(2,1)S(1)} async-done(((bf16[16,32,128]{2,1,0:T(8,128)(2,1)}), bf16[16,32,128]{2,1,0:T(8,128)(2,1)S(1)}, u32[]{:S(2)}, u32[]{:S(2)}) %all-to-all-start.3) | async-done | bytes 131104 | tf_op jit(solution)/shard_map/all_to_all | solution.py:447
  90.7 0.0 copy-done.2
  90.7 1.2 %shard_map.195 = f32[4,8,32,128]{3,2,1,0:T(8,128)} custom-call(bf16[16,32,128]{2,1,0:T(8,128)(2,1)S(1)} %all-to-all-done.3.got, bf16[64,256]{1,0:T(8,128)(2,1)S(1)} %copy-done.2, f32[32,32,128]{2,1,0:T(8,128)S(1)} %shard_map.194.known), custom_call_target="tpu_custom_call" | custom-call | flops 100000000 | bytes 1000000 | tf_op jit(solution)/shard_map/pallas_call | solution.py:448
Async XLA Ops:
  12.1 27.1 %copy-start = (bf16[512,128]{1,0:T(8,128)(2,1)S(1)}, bf16[512,128]{1,0:T(8,128)(2,1)}, u32[]{:S(2)}) copy-start(bf16[512,128]{1,0:T(8,128)(2,1)} %constant.11.clone.phase) | copy-start | bytes 393220
  12.1 40.7 %copy-start.5 = (bf16[32,1,2,2,32,32]{5,4,3,2,1,0:T(8,128)(2,1)S(1)}, bf16[32,1,2,2,32,32]{5,4,3,2,1,0:T(8,128)(2,1)}, u32[]{:S(2)}) copy-start(bf16[32,1,2,2,32,32]{5,4,3,2,1,0:T(8,128)(2,1)} %param.33) | copy-start | bytes 786436
  40.2 21.6 %all-to-all-start.1 = ((f32[32,4,128]{2,1,0:T(4,128)}), f32[32,4,128]{2,1,0:T(4,128)S(1)}, u32[]{:S(2)}, u32[]{:S(2)}) async-start(f32[32,4,128]{2,1,0:T(4,128)} %get-tuple-element.7), calls=%async_computation.1 | async-start | bytes 131072 | tf_op jit(solution)/shard_map/all_to_all | solution.py:426
  52.8 8.9 %copy-start.1 = (bf16[256,64]{1,0:T(8,128)(2,1)S(1)}, bf16[256,64]{1,0:T(8,128)(2,1)}, u32[]{:S(2)}) copy-start(bf16[256,64]{1,0:T(8,128)(2,1)} %constant.13.clone.back) | copy-start | bytes 98308
  52.8 8.9 %copy-start.3 = (bf16[64,256]{1,0:T(8,128)(2,1)S(1)}, bf16[64,256]{1,0:T(8,128)(2,1)}, u32[]{:S(2)}) copy-start(bf16[64,256]{1,0:T(8,128)(2,1)} %constant.12.clone.forward) | copy-start | bytes 98308
  76.1 14.6 %all-to-all-start.3 = ((bf16[16,32,128]{2,1,0:T(8,128)(2,1)}), bf16[16,32,128]{2,1,0:T(8,128)(2,1)S(1)}, u32[]{:S(2)}, u32[]{:S(2)}) async-start(bf16[16,32,128]{2,1,0:T(8,128)(2,1)} %shard_map.193), calls=%async_computation.3 | async-start | bytes 262144 | tf_op jit(solution)/shard_map/all_to_all | solution.py:447
  81.5 0.7 copy-start.6
  82.1 0.7 copy-start.4
  82.8 7.9 %copy-start.2 = (bf16[64,256]{1,0:T(8,128)(2,1)S(1)}, bf16[64,256]{1,0:T(8,128)(2,1)}, u32[]{:S(2)}) copy-start(bf16[64,256]{1,0:T(8,128)(2,1)} %constant.14.clone.inverse) | copy-start | bytes 98308

commit v4 on v3

--- a/solution.py
+++ b/solution.py
@@ -367,7 +367,7 @@
             out[x, y] = 0.5 * (h + h * th)
 
 
-def call(kernel, out_shape, in_specs, scratch=(), flops=0, size=0, vmem=40 * 1024 * 1024):
+def call(kernel, out_shape, in_specs, scratch=(), flops=0, size=0, vmem=8 * 1024 * 1024):
     return pl.pallas_call(
         kernel,
         out_shape=out_shape,
@@ -423,7 +423,15 @@
         [VM, VM],
         flops=100_000_000, size=500_000,
     )(sent, phase_y)
+    known = call(
+        tile_kernel,
+        jax.ShapeDtypeStruct((CX * CY, C, NZ), F32),
+        [SM] + [VM] * 3,
+        [vm((CX * CY * NZ // 4, 4 * C), F32)],
+        flops=100_000_000, size=2_500_000,
+    )(slots, sent, w_point, b_point.reshape(C, 1))
     along_y = lax.all_to_all(along_y, "gx", 0, 0, tiled=True)
+    along_y, known = lax.optimization_barrier((along_y, known))
     lines = call(
         x_kernel,
         jax.ShapeDtypeStruct((N_GX, CX, 128), F32),
@@ -437,13 +445,6 @@
         [VM] * 2,
         flops=100_000_000, size=500_000,
     )(lines, back_y)
-    known = call(
-        tile_kernel,
-        jax.ShapeDtypeStruct((CX * CY, C, NZ), F32),
-        [SM] + [VM] * 3,
-        [vm((CX * CY * NZ // 4, 4 * C), F32)],
-        flops=100_000_000, size=2_500_000,
-    )(slots, sent, w_point, b_point.reshape(C, 1))
     cells = lax.all_to_all(cells, "gy", 0, 0, tiled=True)
     return call(
         end_kernel,

time: 92.4 us -> 92 us (level)
  blocking collectives: 39.5 us -> 59.4 us
  waiting for transfers between devices: 13.8 us -> 5.14 us
  Pallas kernels: 18.1 us -> 11.8 us
  starting transfers between devices: 18 us -> 13.2 us
    all_to_all x0 -> x1, blocking collectives: none -> 13.9 us  [local(): cells = lax.all_to_all(cells, 'gy', 0, 0, tiled=True)]
    all_to_all x1 -> x0, waiting for transfers between devices: 6.01 us -> none  [local(): cells = lax.all_to_all(cells, 'gy', 0, 0, tiled=True)]
    pallas_call x1, Pallas kernels: 12.1 us -> 6.49 us  [stage_one(): call(pair_kernel, jax.ShapeDtypeStruct((N_GY, 16 + BLK * NZ // 4, 128), B...]
    all_to_all x1, blocking collectives: 27.1 us -> 32.7 us  [local(): sent = lax.all_to_all(sent, 'gy', 0, 0, tiled=True)]
    all_to_all x1 -> x0, starting transfers between devices: 5.4 us -> none  [local(): cells = lax.all_to_all(cells, 'gy', 0, 0, tiled=True)]
    all_to_all x1, waiting for transfers between devices: 7.74 us -> 5.14 us  [local(): along_y = lax.all_to_all(along_y, 'gx', 0, 0, tiled=True)]
  transfers between devices with their start and end apart: 2 -> 1, of which waited for: 2 -> 1; matrix products, arithmetic and copies ran while one was open for 1% -> 1% of each run, Pallas kernels for 2% -> 2%
where the time goes in v4:
time: 92 us; the launch traced here: 91.5 us
  blocking collectives  59.4 us (65%)
  starting transfers between devices  13.2 us (14%)
  Pallas kernels  11.8 us (13%)
  waiting for transfers between devices  5.14 us (6%)
  local copies, waits for them, and re-layouts  1.94 us (2%)
    all_to_all x1, blocking collectives, local(): sent = lax.all_to_all(sent, 'gy', 0, 0, tiled=True)  32.7 us
    all_to_all x1, blocking collectives, local(): cells = lax.all_to_all(cells, 'gy', 0, 0, tiled=True)  13.9 us
    all_to_all x1, starting transfers between devices, local(): along_y = lax.all_to_all(along_y, 'gx', 0, 0, tiled=True)  13.2 us
    all_to_all x1, blocking collectives, local(): lines = lax.all_to_all(lines, 'gx', 0, 0, tiled=True)  12.8 us
    pallas_call x1, Pallas kernels, stage_one(): call(pair_kernel, jax.ShapeDtypeStruct((N_GY, 16 + BLK * NZ // 4, 128), B...  6.49 us
    all_to_all x1, waiting for transfers between devices, local(): along_y = lax.all_to_all(along_y, 'gx', 0, 0, tiled=True)  5.14 us
    pallas_call x1, Pallas kernels, local(): call(tile_kernel, jax.ShapeDtypeStruct((CX * CY, C, NZ), F32), [SM] + [VM...  1.84 us
  transfers between devices with their start and end apart: 1, of which 1 were waited for; matrix products, arithmetic and copies ran while one was open for 1% of the time, Pallas kernels for 2%

profile of v4, /device:TPU:1, one launch (start us, length us, event | category | flops | bytes accessed | tf_op | source)
XLA Modules:
  0.0 91.5 jit_solution(4695971824254573276)
XLA Ops:
  0.0 6.5 %shard_map.190 = bf16[16,80,128]{2,1,0:T(8,128)(2,1)} custom-call(s32[2,4]{1,0:T(2,128)} %owner.1, s32[2,4]{1,0:T(2,128)} %tile.1, s32[2]{0:T(128)} %live.1, bf16[32,256]{1,0:T(8,128)(2,1)} %feats.1, bf16[3,256]{1,0:T(4,128)(2,1)} %offs.1, s32[1,256]{1,0:T(1,128)} %bitcast.8, bf16[3,64]{1,0:T(4,128)(2,1)} %bitcast.9, f32[1,64]{1,0:T(1,128)} %bitcast.10, ...), custom_call_target="tpu_custom_call" | custom-call | flops 1600000000 | bytes 1000000 | tf_op jit(solution)/shard_map/pallas_call | solution.py:391
  6.5 0.0 copy-start
  6.5 0.0 copy-start.5
  6.5 32.7 %all_to_all.20.got = bf16[16,80,128]{2,1,0:T(8,128)(2,1)S(1)} all-to-all(bf16[16,80,128]{2,1,0:T(8,128)(2,1)} %shard_map.190), channel_id=1, replica_groups=mesh['gx'=32,'gy'=16] {'gy'}, dimensions={0} | all-to-all | bytes 655360 | tf_op jit(solution)/shard_map/all_to_all | solution.py:419
  39.2 0.0 copy-done
  39.2 1.0 %shard_map.191 = (f32[32,4,128]{2,1,0:T(4,128)}, s32[8,128]{1,0:T(8,128)S(1)}) custom-call(bf16[16,80,128]{2,1,0:T(8,128)(2,1)S(1)} %all_to_all.20.got, bf16[512,128]{1,0:T(8,128)(2,1)S(1)} %copy-done), custom_call_target="tpu_custom_call" | custom-call | flops 100000000 | bytes 500000 | tf_op jit(solution)/shard_map/pallas_call | solution.py:420
  40.2 13.2 %all-to-all-start.1 = ((f32[32,4,128]{2,1,0:T(4,128)}), f32[32,4,128]{2,1,0:T(4,128)S(1)}, u32[]{:S(2)}, u32[]{:S(2)}) async-start(f32[32,4,128]{2,1,0:T(4,128)} %get-tuple-element.9), calls=%async_computation.1 | async-start | bytes 131072 | tf_op jit(solution)/shard_map/all_to_all | solution.py:433
  53.4 0.0 copy-start.6
  53.4 0.6 copy-done.6
  54.0 0.1 copy.21.bias
  54.1 0.0 copy-done.5
  54.1 0.0 copy-start.4
  54.1 1.2 %reshape.19.weights = bf16[32,4096]{1,0:T(8,128)(2,1)S(1)} reshape(bf16[32,1,2,2,32,32]{5,4,3,2,1,0:T(8,128)(2,1)S(1)} %copy-done.5) | data formatting | bytes 524288 | tf_op jit(solution)/shard_map/reshape | solution.py:440
  55.3 0.0 copy-done.4
  55.3 0.0 copy-start.1
  55.3 0.0 copy-start.3
  55.3 1.8 %shard_map.192.known = f32[32,32,128]{2,1,0:T(8,128)S(1)} custom-call(s32[8,128]{1,0:T(8,128)S(1)} %get-tuple-element.10.slots, bf16[16,80,128]{2,1,0:T(8,128)(2,1)S(1)} %all_to_all.20.got, bf16[32,32]{1,0:T(8,128)(2,1)S(1)} %copy-done.4, f32[32,1]{1,0:T(8,128)S(1)} %copy.21.bias), custom_call_target="tpu_custom_call" | custom-call | flops 100000000 | bytes 2500000 | tf_op jit(solution)/shard_map/pallas_call | solution.py:426
  57.2 5.1 %all-to-all-done.1.got = f32[32,4,128]{2,1,0:T(4,128)S(1)} async-done(((f32[32,4,128]{2,1,0:T(4,128)}), f32[32,4,128]{2,1,0:T(4,128)S(1)}, u32[]{:S(2)}, u32[]{:S(2)}) %all-to-all-start.1) | async-done | bytes 65568 | tf_op jit(solution)/shard_map/all_to_all | solution.py:433
  62.3 0.0 copy-done.1
  62.3 0.0 copy-done.3
  62.3 0.9 %shard_map.193 = f32[32,4,128]{2,1,0:T(4,128)S(1)} custom-call(f32[32,4,128]{2,1,0:T(4,128)S(1)} %all-to-all-done.1.got, bf16[32,4096]{1,0:T(8,128)(2,1)S(1)} %reshape.19.weights, bf16[64,256]{1,0:T(8,128)(2,1)S(1)} %copy-done.3, bf16[256,64]{1,0:T(8,128)(2,1)S(1)} %copy-done.1), custom_call_target="tpu_custom_call" | custom-call | flops 100000000 | bytes 500000 | tf_op jit(solution)/shard_map/pallas_call | solution.py:435
  63.3 12.8 %all_to_all.21.got = f32[32,4,128]{2,1,0:T(4,128)S(1)} all-to-all(f32[32,4,128]{2,1,0:T(4,128)S(1)} %shard_map.193), channel_id=1, replica_groups=mesh['gx'=32,'gy'=16] {'gx'}, dimensions={0} | all-to-all | bytes 131072 | tf_op jit(solution)/shard_map/all_to_all | solution.py:441
  76.1 0.4 shard_map.194
  76.4 0.0 copy-start.2
  76.4 13.9 %all_to_all.22.got = bf16[16,32,128]{2,1,0:T(8,128)(2,1)S(1)} all-to-all(bf16[16,32,128]{2,1,0:T(8,128)(2,1)S(1)} %shard_map.194), channel_id=1, replica_groups=mesh['gx'=32,'gy'=16] {'gy'}, dimensions={0} | all-to-all | bytes 262144 | tf_op jit(solution)/shard_map/all_to_all | solution.py:448
  90.3 0.0 copy-done.2
  90.3 1.2 %shard_map.195 = f32[4,8,32,128]{3,2,1,0:T(8,128)} custom-call(bf16[16,32,128]{2,1,0:T(8,128)(2,1)S(1)} %all_to_all.22.got, bf16[64,256]{1,0:T(8,128)(2,1)S(1)} %copy-done.2, f32[32,32,128]{2,1,0:T(8,128)S(1)} %shard_map.192.known), custom_call_target="tpu_custom_call" | custom-call | flops 100000000 | bytes 1000000 | tf_op jit(solution)/shard_map/pallas_call | solution.py:449
Async XLA Ops:
  6.5 32.7 %copy-start = (bf16[512,128]{1,0:T(8,128)(2,1)S(1)}, bf16[512,128]{1,0:T(8,128)(2,1)}, u32[]{:S(2)}) copy-start(bf16[512,128]{1,0:T(8,128)(2,1)} %constant.11.clone.phase) | copy-start | bytes 393220
  6.5 47.6 %copy-start.5 = (bf16[32,1,2,2,32,32]{5,4,3,2,1,0:T(8,128)(2,1)S(1)}, bf16[32,1,2,2,32,32]{5,4,3,2,1,0:T(8,128)(2,1)}, u32[]{:S(2)}) copy-start(bf16[32,1,2,2,32,32]{5,4,3,2,1,0:T(8,128)(2,1)} %param.33) | copy-start | bytes 786436
  40.2 22.1 %all-to-all-start.1 = ((f32[32,4,128]{2,1,0:T(4,128)}), f32[32,4,128]{2,1,0:T(4,128)S(1)}, u32[]{:S(2)}, u32[]{:S(2)}) async-start(f32[32,4,128]{2,1,0:T(4,128)} %get-tuple-element.9), calls=%async_computation.1 | async-start | bytes 131072 | tf_op jit(solution)/shard_map/all_to_all | solution.py:433
  53.4 0.7 copy-start.6
  54.1 1.2 %copy-start.4 = (bf16[32,32]{1,0:T(8,128)(2,1)S(1)}, bf16[32,32]{1,0:T(8,128)(2,1)}, u32[]{:S(2)}) copy-start(bf16[32,32]{1,0:T(8,128)(2,1)} %wp.1) | copy-start | bytes 6148
  55.3 7.0 %copy-start.1 = (bf16[256,64]{1,0:T(8,128)(2,1)S(1)}, bf16[256,64]{1,0:T(8,128)(2,1)}, u32[]{:S(2)}) copy-start(bf16[256,64]{1,0:T(8,128)(2,1)} %constant.13.clone.back) | copy-start | bytes 98308
  55.3 7.0 %copy-start.3 = (bf16[64,256]{1,0:T(8,128)(2,1)S(1)}, bf16[64,256]{1,0:T(8,128)(2,1)}, u32[]{:S(2)}) copy-start(bf16[64,256]{1,0:T(8,128)(2,1)} %constant.12.clone.forward) | copy-start | bytes 98308
  76.4 13.9 %copy-start.2 = (bf16[64,256]{1,0:T(8,128)(2,1)S(1)}, bf16[64,256]{1,0:T(8,128)(2,1)}, u32[]{:S(2)}) copy-start(bf16[64,256]{1,0:T(8,128)(2,1)} %constant.14.clone.inverse) | copy-start | bytes 98308

commit v5 on v4

--- a/solution.py
+++ b/solution.py
@@ -285,7 +285,8 @@
     turned = dot(phase[...], hot)
     here = (iota((512, 128), 0) & (CX - 1)).astype(F32) == xs
     turned = jnp.where(here, turned, 0.0).astype(BF16)
-    both = dot(turned[:256], values.astype(BF16)) + dot(turned[256:], rotated(values, 1.0).astype(BF16))
+    turned = jnp.concatenate([turned[:256], turned[256:]], axis=1)
+    both = dot(turned, jnp.concatenate([values, rotated(values, 1.0)], axis=0).astype(BF16))
     result = both[:128] + both[128:]
     out[...] = result.reshape(MODES, CX, 128).astype(out.dtype)
     yi = ys.astype(jnp.int32)
@@ -307,9 +308,9 @@
     values = got[...].astype(F32).reshape(size_x, 128)
     spectrum = table_dot(forward[...], jnp.concatenate([values, rotated(values, 1.0)], axis=0))
     parts = [spectrum if g == 0 else pltpu.roll(spectrum, 128 - g * C, 1) for g in range(4)]
-    high, low = halves(jnp.concatenate(parts, axis=0))
-    spread = ((iota((128, C * C), 1) // C) == iota((128, C * C), 0)).astype(BF16)
-    wide = dot(high, spread) + dot(low, spread)
+    terms = jnp.concatenate(halves(jnp.concatenate(parts, axis=0)), axis=1)
+    spread = ((iota((256, C * C), 1) // C) == (iota((256, C * C), 0) & 127)).astype(BF16)
+    wide = dot(terms, spread)
     totals = []
     for k in range(2):
         real = wide[(2 * k) * MODES : (2 * k + 1) * MODES]
@@ -355,8 +356,9 @@
         out[:, g * CY : (g + 1) * CY, :] = piece.astype(out.dtype)
 
 
-def end_kernel(got, inverse, known, out, wide):
+def end_kernel(got, inverse, known, out, wide, done, sent):
     wide[...] = got[...].astype(F32).reshape(N_GY * 4 * CY, 128)
+    copies = []
     for y in range(CY):
         values = wide[pl.ds(y, 4 * N_GY, stride=CY), :].astype(BF16)
         both = dot(values, inverse[...], TN)
@@ -364,14 +366,19 @@
         for x in range(CX):
             h = line[x * C : (x + 1) * C] + known[x * CY + y]
             th = jnp.tanh(h * (GELU_B * (h * h) + GELU_A))
-            out[x, y] = 0.5 * (h + h * th)
-
-
-def call(kernel, out_shape, in_specs, scratch=(), flops=0, size=0, vmem=8 * 1024 * 1024):
+            done[y, x] = 0.5 * (h + h * th)
+        copies.append(pltpu.make_async_copy(done.at[y], out.at[:, y], sent.at[y]))
+        copies[-1].start()
+    for copy in copies:
+        copy.wait()
+
+
+def call(kernel, out_shape, in_specs, scratch=(), flops=0, size=0, vmem=8 * 1024 * 1024, out=None):
     return pl.pallas_call(
         kernel,
         out_shape=out_shape,
         in_specs=in_specs,
+        **({} if out is None else {"out_specs": out}),
         scratch_shapes=list(scratch),
         compiler_params=pltpu.CompilerParams(vmem_limit_bytes=vmem),
         cost_estimate=pl.CostEstimate(flops=flops, bytes_accessed=size, transcendentals=0),
@@ -450,8 +457,8 @@
         end_kernel,
         jax.ShapeDtypeStruct((CX, CY, C, NZ), F32),
         [VM] * 3,
-        [vm((N_GY * 4 * CY, 128), F32)],
-        flops=100_000_000, size=1_000_000,
+        [vm((N_GY * 4 * CY, 128), F32), vm((CY, CX, C, NZ), F32), pltpu.SemaphoreType.DMA((CY,))],
+        flops=100_000_000, size=1_000_000, out=pl.BlockSpec(memory_space=pl.ANY),
     )(cells, inverse_z, known)
 
 

time: 92 us -> 91.4 us (level)
  blocking collectives: 59.4 us -> 53.8 us
  Pallas kernels: 11.8 us -> 15.4 us
  starting transfers between devices: 13.2 us -> 14.2 us
    all_to_all x1, blocking collectives: 32.7 us -> 27.1 us  [local(): sent = lax.all_to_all(sent, 'gy', 0, 0, tiled=True)]
    pallas_call x1, Pallas kernels: 6.49 us -> 10.2 us  [stage_one(): call(pair_kernel, jax.ShapeDtypeStruct((N_GY, 16 + BLK * NZ // 4, 128), B...]
    all_to_all x1, starting transfers between devices: 13.2 us -> 14.2 us  [local(): along_y = lax.all_to_all(along_y, 'gx', 0, 0, tiled=True)]
where the time goes in v5:
time: 91.4 us; the launch traced here: 90.5 us
  blocking collectives  53.8 us (59%)
  Pallas kernels  15.4 us (17%)
  starting transfers between devices  14.2 us (16%)
  waiting for transfers between devices  5.14 us (6%)
  local copies, waits for them, and re-layouts  1.94 us (2%)
    all_to_all x1, blocking collectives, local(): sent = lax.all_to_all(sent, 'gy', 0, 0, tiled=True)  27.1 us
    all_to_all x1, starting transfers between devices, local(): along_y = lax.all_to_all(along_y, 'gx', 0, 0, tiled=True)  14.2 us
    all_to_all x1, blocking collectives, local(): cells = lax.all_to_all(cells, 'gy', 0, 0, tiled=True)  13.9 us
    all_to_all x1, blocking collectives, local(): lines = lax.all_to_all(lines, 'gx', 0, 0, tiled=True)  12.8 us
    pallas_call x1, Pallas kernels, stage_one(): call(pair_kernel, jax.ShapeDtypeStruct((N_GY, 16 + BLK * NZ // 4, 128), B...  10.2 us
    all_to_all x1, waiting for transfers between devices, local(): along_y = lax.all_to_all(along_y, 'gx', 0, 0, tiled=True)  5.14 us
    pallas_call x1, Pallas kernels, local(): call(tile_kernel, jax.ShapeDtypeStruct((CX * CY, C, NZ), F32), [SM] + [VM...  1.84 us
  transfers between devices with their start and end apart: 1, of which 1 were waited for; matrix products, arithmetic and copies ran while one was open for 1% of the time, Pallas kernels for 2%

profile of v5, /device:TPU:1, one launch (start us, length us, event | category | flops | bytes accessed | tf_op | source)
XLA Modules:
  0.0 90.5 jit_solution(689011074647421388)
XLA Ops:
  0.0 10.2 %shard_map.190 = bf16[16,80,128]{2,1,0:T(8,128)(2,1)} custom-call(s32[2,4]{1,0:T(2,128)} %owner.1, s32[2,4]{1,0:T(2,128)} %tile.1, s32[2]{0:T(128)} %live.1, bf16[32,256]{1,0:T(8,128)(2,1)} %feats.1, bf16[3,256]{1,0:T(4,128)(2,1)} %offs.1, s32[1,256]{1,0:T(1,128)} %bitcast.8, bf16[3,64]{1,0:T(4,128)(2,1)} %bitcast.9, f32[1,64]{1,0:T(1,128)} %bitcast.10, ...), custom_call_target="tpu_custom_call" | custom-call | flops 1600000000 | bytes 1000000 | tf_op jit(solution)/shard_map/pallas_call | solution.py:398
  10.2 0.0 copy-start
  10.2 0.0 copy-start.5
  10.2 27.1 %all_to_all.20.got = bf16[16,80,128]{2,1,0:T(8,128)(2,1)S(1)} all-to-all(bf16[16,80,128]{2,1,0:T(8,128)(2,1)} %shard_map.190), channel_id=1, replica_groups=mesh['gx'=32,'gy'=16] {'gy'}, dimensions={0} | all-to-all | bytes 655360 | tf_op jit(solution)/shard_map/all_to_all | solution.py:426
  37.3 0.0 copy-done
  37.3 1.0 %shard_map.191 = (f32[32,4,128]{2,1,0:T(4,128)}, s32[8,128]{1,0:T(8,128)S(1)}) custom-call(bf16[16,80,128]{2,1,0:T(8,128)(2,1)S(1)} %all_to_all.20.got, bf16[512,128]{1,0:T(8,128)(2,1)S(1)} %copy-done), custom_call_target="tpu_custom_call" | custom-call | flops 100000000 | bytes 500000 | tf_op jit(solution)/shard_map/pallas_call | solution.py:427
  38.3 14.2 %all-to-all-start.1 = ((f32[32,4,128]{2,1,0:T(4,128)}), f32[32,4,128]{2,1,0:T(4,128)S(1)}, u32[]{:S(2)}, u32[]{:S(2)}) async-start(f32[32,4,128]{2,1,0:T(4,128)} %get-tuple-element.9), calls=%async_computation.1 | async-start | bytes 131072 | tf_op jit(solution)/shard_map/all_to_all | solution.py:440
  52.6 0.0 copy-start.6
  52.6 0.6 copy-done.6
  53.2 0.1 copy.21.bias
  53.3 0.0 copy-done.5
  53.3 0.0 copy-start.4
  53.3 1.2 %reshape.19.weights = bf16[32,4096]{1,0:T(8,128)(2,1)S(1)} reshape(bf16[32,1,2,2,32,32]{5,4,3,2,1,0:T(8,128)(2,1)S(1)} %copy-done.5) | data formatting | bytes 524288 | tf_op jit(solution)/shard_map/reshape | solution.py:447
  54.5 0.0 copy-done.4
  54.5 0.0 copy-start.1
  54.5 0.0 copy-start.3
  54.5 1.8 %shard_map.192.known = f32[32,32,128]{2,1,0:T(8,128)S(1)} custom-call(s32[8,128]{1,0:T(8,128)S(1)} %get-tuple-element.10.slots, bf16[16,80,128]{2,1,0:T(8,128)(2,1)S(1)} %all_to_all.20.got, bf16[32,32]{1,0:T(8,128)(2,1)S(1)} %copy-done.4, f32[32,1]{1,0:T(8,128)S(1)} %copy.21.bias), custom_call_target="tpu_custom_call" | custom-call | flops 100000000 | bytes 2500000 | tf_op jit(solution)/shard_map/pallas_call | solution.py:433
  56.4 5.1 %all-to-all-done.1.got = f32[32,4,128]{2,1,0:T(4,128)S(1)} async-done(((f32[32,4,128]{2,1,0:T(4,128)}), f32[32,4,128]{2,1,0:T(4,128)S(1)}, u32[]{:S(2)}, u32[]{:S(2)}) %all-to-all-start.1) | async-done | bytes 65568 | tf_op jit(solution)/shard_map/all_to_all | solution.py:440
  61.5 0.0 copy-done.1
  61.5 0.0 copy-done.3
  61.5 0.8 shard_map.193
  62.4 12.8 %all_to_all.21.got = f32[32,4,128]{2,1,0:T(4,128)S(1)} all-to-all(f32[32,4,128]{2,1,0:T(4,128)S(1)} %shard_map.193), channel_id=1, replica_groups=mesh['gx'=32,'gy'=16] {'gx'}, dimensions={0} | all-to-all | bytes 131072 | tf_op jit(solution)/shard_map/all_to_all | solution.py:448
  75.2 0.4 shard_map.194
  75.5 0.0 copy-start.2
  75.5 13.9 %all_to_all.22.got = bf16[16,32,128]{2,1,0:T(8,128)(2,1)S(1)} all-to-all(bf16[16,32,128]{2,1,0:T(8,128)(2,1)S(1)} %shard_map.194), channel_id=1, replica_groups=mesh['gx'=32,'gy'=16] {'gy'}, dimensions={0} | all-to-all | bytes 262144 | tf_op jit(solution)/shard_map/all_to_all | solution.py:455
  89.4 0.0 copy-done.2
  89.4 1.1 %shard_map.195 = f32[4,8,32,128]{3,2,1,0:T(8,128)} custom-call(bf16[16,32,128]{2,1,0:T(8,128)(2,1)S(1)} %all_to_all.22.got, bf16[64,256]{1,0:T(8,128)(2,1)S(1)} %copy-done.2, f32[32,32,128]{2,1,0:T(8,128)S(1)} %shard_map.192.known), custom_call_target="tpu_custom_call" | custom-call | flops 100000000 | bytes 1000000 | tf_op jit(solution)/shard_map/pallas_call | solution.py:456
Async XLA Ops:
  10.2 27.1 %copy-start = (bf16[512,128]{1,0:T(8,128)(2,1)S(1)}, bf16[512,128]{1,0:T(8,128)(2,1)}, u32[]{:S(2)}) copy-start(bf16[512,128]{1,0:T(8,128)(2,1)} %constant.11.clone.phase) | copy-start | bytes 393220
  10.2 43.1 %copy-start.5 = (bf16[32,1,2,2,32,32]{5,4,3,2,1,0:T(8,128)(2,1)S(1)}, bf16[32,1,2,2,32,32]{5,4,3,2,1,0:T(8,128)(2,1)}, u32[]{:S(2)}) copy-start(bf16[32,1,2,2,32,32]{5,4,3,2,1,0:T(8,128)(2,1)} %param.33) | copy-start | bytes 786436
  38.3 23.2 %all-to-all-start.1 = ((f32[32,4,128]{2,1,0:T(4,128)}), f32[32,4,128]{2,1,0:T(4,128)S(1)}, u32[]{:S(2)}, u32[]{:S(2)}) async-start(f32[32,4,128]{2,1,0:T(4,128)} %get-tuple-element.9), calls=%async_computation.1 | async-start | bytes 131072 | tf_op jit(solution)/shard_map/all_to_all | solution.py:440
  52.6 0.7 copy-start.6
  53.3 1.2 %copy-start.4 = (bf16[32,32]{1,0:T(8,128)(2,1)S(1)}, bf16[32,32]{1,0:T(8,128)(2,1)}, u32[]{:S(2)}) copy-start(bf16[32,32]{1,0:T(8,128)(2,1)} %wp.1) | copy-start | bytes 6148
  54.5 7.0 %copy-start.1 = (bf16[256,64]{1,0:T(8,128)(2,1)S(1)}, bf16[256,64]{1,0:T(8,128)(2,1)}, u32[]{:S(2)}) copy-start(bf16[256,64]{1,0:T(8,128)(2,1)} %constant.13.clone.back) | copy-start | bytes 98308
  54.5 7.0 %copy-start.3 = (bf16[64,256]{1,0:T(8,128)(2,1)S(1)}, bf16[64,256]{1,0:T(8,128)(2,1)}, u32[]{:S(2)}) copy-start(bf16[64,256]{1,0:T(8,128)(2,1)} %constant.12.clone.forward) | copy-start | bytes 98308
  75.5 13.9 %copy-start.2 = (bf16[64,256]{1,0:T(8,128)(2,1)S(1)}, bf16[64,256]{1,0:T(8,128)(2,1)}, u32[]{:S(2)}) copy-start(bf16[64,256]{1,0:T(8,128)(2,1)} %constant.14.clone.inverse) | copy-start | bytes 98308

commit v6 on v4

--- a/solution.py
+++ b/solution.py
@@ -22,7 +22,7 @@
 LIST = 4
 PAIRS = BLK * LIST
 MODES = 32
-ANCHOR = 16
+ANCHOR = 32
 VMEM_ONE = 62 * 1024 * 1024
 F32 = jnp.float32
 BF16 = jnp.bfloat16
@@ -195,13 +195,16 @@
     lane_group = iota((N_GY, 4 * C), 1) // C
     held[...] = jnp.zeros_like(held)
     table = fz[...]
-    for j in range(PAIRS):
-        both = dot(table, by_cell[0][j])
-        full = both[: 4 * N_GY] + both[4 * N_GY :] + dot(table[: 4 * N_GY], by_cell[1][j])
-        picked = jnp.zeros((N_GY, 4 * C), F32)
-        for g in range(4):
-            picked = jnp.where(lane_group == g, full[g * N_GY : (g + 1) * N_GY], picked)
-        held[:, j, :] = picked
+    for j in range(0, PAIRS, 2):
+        high, low = (jnp.concatenate(term[j : j + 2], axis=1) for term in by_cell)
+        both = dot(table, high)
+        full = both[: 4 * N_GY] + both[4 * N_GY :] + dot(table[: 4 * N_GY], low)
+        for k in range(2):
+            picked = jnp.zeros((N_GY, 4 * C), F32)
+            for g in range(4):
+                part = full[g * N_GY : (g + 1) * N_GY, k * 4 * C : (k + 1) * 4 * C]
+                picked = jnp.where(lane_group == g, part, picked)
+            held[:, j + k, :] = picked
     lane = iota((1, 128), 1)
     xs = jnp.zeros((1, 128), jnp.int32)
     ys = jnp.zeros((1, 128), jnp.int32)
@@ -285,7 +288,8 @@
     turned = dot(phase[...], hot)
     here = (iota((512, 128), 0) & (CX - 1)).astype(F32) == xs
     turned = jnp.where(here, turned, 0.0).astype(BF16)
-    both = dot(turned[:256], values.astype(BF16)) + dot(turned[256:], rotated(values, 1.0).astype(BF16))
+    turned = jnp.concatenate([turned[:256], turned[256:]], axis=1)
+    both = dot(turned, jnp.concatenate([values, rotated(values, 1.0)], axis=0).astype(BF16))
     result = both[:128] + both[128:]
     out[...] = result.reshape(MODES, CX, 128).astype(out.dtype)
     yi = ys.astype(jnp.int32)
@@ -307,9 +311,9 @@
     values = got[...].astype(F32).reshape(size_x, 128)
     spectrum = table_dot(forward[...], jnp.concatenate([values, rotated(values, 1.0)], axis=0))
     parts = [spectrum if g == 0 else pltpu.roll(spectrum, 128 - g * C, 1) for g in range(4)]
-    high, low = halves(jnp.concatenate(parts, axis=0))
-    spread = ((iota((128, C * C), 1) // C) == iota((128, C * C), 0)).astype(BF16)
-    wide = dot(high, spread) + dot(low, spread)
+    terms = jnp.concatenate(halves(jnp.concatenate(parts, axis=0)), axis=1)
+    spread = ((iota((256, C * C), 1) // C) == (iota((256, C * C), 0) & 127)).astype(BF16)
+    wide = dot(terms, spread)
     totals = []
     for k in range(2):
         real = wide[(2 * k) * MODES : (2 * k + 1) * MODES]

time: 92 us -> 91.6 us (level)
  blocking collectives: 59.4 us -> 47.9 us
  Pallas kernels: 11.8 us -> 19.1 us
  starting transfers between devices: 13.2 us -> 17.2 us
    all_to_all x1, blocking collectives: 32.7 us -> 21.3 us  [local(): sent = lax.all_to_all(sent, 'gy', 0, 0, tiled=True)]
    pallas_call x1, Pallas kernels: 6.49 us -> 13.9 us  [stage_one(): call(pair_kernel, jax.ShapeDtypeStruct((N_GY, 16 + BLK * NZ // 4, 128), B...]
    all_to_all x1, starting transfers between devices: 13.2 us -> 17.2 us  [local(): along_y = lax.all_to_all(along_y, 'gx', 0, 0, tiled=True)]
where the time goes in v6:
time: 91.6 us; the launch traced here: 91.4 us
  blocking collectives  47.9 us (52%)
  Pallas kernels  19.1 us (21%)
  starting transfers between devices  17.2 us (19%)
  waiting for transfers between devices  5.14 us (6%)
  local copies, waits for them, and re-layouts  1.94 us (2%)
    all_to_all x1, blocking collectives, local(): sent = lax.all_to_all(sent, 'gy', 0, 0, tiled=True)  21.3 us
    all_to_all x1, starting transfers between devices, local(): along_y = lax.all_to_all(along_y, 'gx', 0, 0, tiled=True)  17.2 us
    pallas_call x1, Pallas kernels, stage_one(): call(pair_kernel, jax.ShapeDtypeStruct((N_GY, 16 + BLK * NZ // 4, 128), B...  13.9 us
    all_to_all x1, blocking collectives, local(): cells = lax.all_to_all(cells, 'gy', 0, 0, tiled=True)  13.9 us
    all_to_all x1, blocking collectives, local(): lines = lax.all_to_all(lines, 'gx', 0, 0, tiled=True)  12.8 us
    all_to_all x1, waiting for transfers between devices, local(): along_y = lax.all_to_all(along_y, 'gx', 0, 0, tiled=True)  5.14 us
    pallas_call x1, Pallas kernels, local(): call(tile_kernel, jax.ShapeDtypeStruct((CX * CY, C, NZ), F32), [SM] + [VM...  1.84 us
  transfers between devices with their start and end apart: 1, of which 1 were waited for; matrix products, arithmetic and copies ran while one was open for 1% of the time, Pallas kernels for 2%

profile of v6, /device:TPU:1, one launch (start us, length us, event | category | flops | bytes accessed | tf_op | source)
XLA Modules:
  0.0 91.4 jit_solution(8853633054990030605)
XLA Ops:
  0.0 13.9 %shard_map.190 = bf16[16,80,128]{2,1,0:T(8,128)(2,1)} custom-call(s32[2,4]{1,0:T(2,128)} %owner.1, s32[2,4]{1,0:T(2,128)} %tile.1, s32[2]{0:T(128)} %live.1, bf16[32,256]{1,0:T(8,128)(2,1)} %feats.1, bf16[3,256]{1,0:T(4,128)(2,1)} %offs.1, s32[1,256]{1,0:T(1,128)} %bitcast.8, bf16[3,64]{1,0:T(4,128)(2,1)} %bitcast.9, f32[1,64]{1,0:T(1,128)} %bitcast.10, ...), custom_call_target="tpu_custom_call" | custom-call | flops 1600000000 | bytes 1000000 | tf_op jit(solution)/shard_map/pallas_call | solution.py:395
  13.9 0.0 copy-start
  13.9 0.0 copy-start.5
  13.9 21.3 %all_to_all.20.got = bf16[16,80,128]{2,1,0:T(8,128)(2,1)S(1)} all-to-all(bf16[16,80,128]{2,1,0:T(8,128)(2,1)} %shard_map.190), channel_id=1, replica_groups=mesh['gx'=32,'gy'=16] {'gy'}, dimensions={0} | all-to-all | bytes 655360 | tf_op jit(solution)/shard_map/all_to_all | solution.py:423
  35.1 0.0 copy-done
  35.2 1.0 %shard_map.191 = (f32[32,4,128]{2,1,0:T(4,128)}, s32[8,128]{1,0:T(8,128)S(1)}) custom-call(bf16[16,80,128]{2,1,0:T(8,128)(2,1)S(1)} %all_to_all.20.got, bf16[512,128]{1,0:T(8,128)(2,1)S(1)} %copy-done), custom_call_target="tpu_custom_call" | custom-call | flops 100000000 | bytes 500000 | tf_op jit(solution)/shard_map/pallas_call | solution.py:424
  36.2 17.2 %all-to-all-start.1 = ((f32[32,4,128]{2,1,0:T(4,128)}), f32[32,4,128]{2,1,0:T(4,128)S(1)}, u32[]{:S(2)}, u32[]{:S(2)}) async-start(f32[32,4,128]{2,1,0:T(4,128)} %get-tuple-element.9), calls=%async_computation.1 | async-start | bytes 131072 | tf_op jit(solution)/shard_map/all_to_all | solution.py:437
  53.3 0.0 copy-start.6
  53.3 0.6 copy-done.6
  54.0 0.1 copy.21.bias
  54.1 0.0 copy-done.5
  54.1 0.0 copy-start.4
  54.1 1.2 %reshape.19.weights = bf16[32,4096]{1,0:T(8,128)(2,1)S(1)} reshape(bf16[32,1,2,2,32,32]{5,4,3,2,1,0:T(8,128)(2,1)S(1)} %copy-done.5) | data formatting | bytes 524288 | tf_op jit(solution)/shard_map/reshape | solution.py:444
  55.3 0.0 copy-done.4
  55.3 0.0 copy-start.1
  55.3 0.0 copy-start.3
  55.3 1.8 %shard_map.192.known = f32[32,32,128]{2,1,0:T(8,128)S(1)} custom-call(s32[8,128]{1,0:T(8,128)S(1)} %get-tuple-element.10.slots, bf16[16,80,128]{2,1,0:T(8,128)(2,1)S(1)} %all_to_all.20.got, bf16[32,32]{1,0:T(8,128)(2,1)S(1)} %copy-done.4, f32[32,1]{1,0:T(8,128)S(1)} %copy.21.bias), custom_call_target="tpu_custom_call" | custom-call | flops 100000000 | bytes 2500000 | tf_op jit(solution)/shard_map/pallas_call | solution.py:430
  57.1 5.1 %all-to-all-done.1.got = f32[32,4,128]{2,1,0:T(4,128)S(1)} async-done(((f32[32,4,128]{2,1,0:T(4,128)}), f32[32,4,128]{2,1,0:T(4,128)S(1)}, u32[]{:S(2)}, u32[]{:S(2)}) %all-to-all-start.1) | async-done | bytes 65568 | tf_op jit(solution)/shard_map/all_to_all | solution.py:437
  62.3 0.0 copy-done.1
  62.3 0.0 copy-done.3
  62.3 0.8 shard_map.193
  63.1 12.8 %all_to_all.21.got = f32[32,4,128]{2,1,0:T(4,128)S(1)} all-to-all(f32[32,4,128]{2,1,0:T(4,128)S(1)} %shard_map.193), channel_id=1, replica_groups=mesh['gx'=32,'gy'=16] {'gx'}, dimensions={0} | all-to-all | bytes 131072 | tf_op jit(solution)/shard_map/all_to_all | solution.py:445
  75.9 0.4 shard_map.194
  76.3 0.0 copy-start.2
  76.3 13.9 %all_to_all.22.got = bf16[16,32,128]{2,1,0:T(8,128)(2,1)S(1)} all-to-all(bf16[16,32,128]{2,1,0:T(8,128)(2,1)S(1)} %shard_map.194), channel_id=1, replica_groups=mesh['gx'=32,'gy'=16] {'gy'}, dimensions={0} | all-to-all | bytes 262144 | tf_op jit(solution)/shard_map/all_to_all | solution.py:452
  90.2 0.0 copy-done.2
  90.2 1.2 %shard_map.195 = f32[4,8,32,128]{3,2,1,0:T(8,128)} custom-call(bf16[16,32,128]{2,1,0:T(8,128)(2,1)S(1)} %all_to_all.22.got, bf16[64,256]{1,0:T(8,128)(2,1)S(1)} %copy-done.2, f32[32,32,128]{2,1,0:T(8,128)S(1)} %shard_map.192.known), custom_call_target="tpu_custom_call" | custom-call | flops 100000000 | bytes 1000000 | tf_op jit(solution)/shard_map/pallas_call | solution.py:453
Async XLA Ops:
  13.9 21.3 %copy-start = (bf16[512,128]{1,0:T(8,128)(2,1)S(1)}, bf16[512,128]{1,0:T(8,128)(2,1)}, u32[]{:S(2)}) copy-start(bf16[512,128]{1,0:T(8,128)(2,1)} %constant.11.clone.phase) | copy-start | bytes 393220
  13.9 40.2 %copy-start.5 = (bf16[32,1,2,2,32,32]{5,4,3,2,1,0:T(8,128)(2,1)S(1)}, bf16[32,1,2,2,32,32]{5,4,3,2,1,0:T(8,128)(2,1)}, u32[]{:S(2)}) copy-start(bf16[32,1,2,2,32,32]{5,4,3,2,1,0:T(8,128)(2,1)} %param.33) | copy-start | bytes 786436
  36.2 26.1 %all-to-all-start.1 = ((f32[32,4,128]{2,1,0:T(4,128)}), f32[32,4,128]{2,1,0:T(4,128)S(1)}, u32[]{:S(2)}, u32[]{:S(2)}) async-start(f32[32,4,128]{2,1,0:T(4,128)} %get-tuple-element.9), calls=%async_computation.1 | async-start | bytes 131072 | tf_op jit(solution)/shard_map/all_to_all | solution.py:437
  53.3 0.7 copy-start.6
  54.1 1.2 %copy-start.4 = (bf16[32,32]{1,0:T(8,128)(2,1)S(1)}, bf16[32,32]{1,0:T(8,128)(2,1)}, u32[]{:S(2)}) copy-start(bf16[32,32]{1,0:T(8,128)(2,1)} %wp.1) | copy-start | bytes 6148
  55.3 7.0 %copy-start.1 = (bf16[256,64]{1,0:T(8,128)(2,1)S(1)}, bf16[256,64]{1,0:T(8,128)(2,1)}, u32[]{:S(2)}) copy-start(bf16[256,64]{1,0:T(8,128)(2,1)} %constant.13.clone.back) | copy-start | bytes 98308
  55.3 7.0 %copy-start.3 = (bf16[64,256]{1,0:T(8,128)(2,1)S(1)}, bf16[64,256]{1,0:T(8,128)(2,1)}, u32[]{:S(2)}) copy-start(bf16[64,256]{1,0:T(8,128)(2,1)} %constant.12.clone.forward) | copy-start | bytes 98308
  76.3 13.9 %copy-start.2 = (bf16[64,256]{1,0:T(8,128)(2,1)S(1)}, bf16[64,256]{1,0:T(8,128)(2,1)}, u32[]{:S(2)}) copy-start(bf16[64,256]{1,0:T(8,128)(2,1)} %constant.14.clone.inverse) | copy-start | bytes 98308
